TPU v7x, 256 devices: a whole 4x4x8 slice. The times are simulated.
256 devices in a mesh: blk: 64 (over z, x, y_lo), rep: 4 (over y_hi, core).
Axes of the slice: x: 4, y: 4 (y_hi: 2, y_lo: 2; y = y_hi * 2 + y_lo), z: 8, core: 2. Of those that a mesh axis runs over, the one named last changes fastest.
Arguments:
- row_emb: bfloat16 [65536, 300], P('blk'), may hold values from -1.796875 to 1.796875
- col_emb: bfloat16 [65536, 300], P('blk'), may hold values from -1.796875 to 1.796875
- row_acc: float32 [65536, 300], P('blk'), may hold values from 0.0003 to 0.03
- col_acc: float32 [65536, 300], P('blk'), may hold values from 0.0003 to 0.03
- row_offset: bfloat16 [65536], P('blk'), may hold values from 0.5 to 3
- col_offset: bfloat16 [65536], P('blk'), may hold values from 0.5 to 3
- counts: int32 [64, 4, 2, 1024, 1024], P('blk', 'rep'), may hold values from 0 to 1023, as said below
- row_index: int32 [64, 4, 2, 1024], P('blk', 'rep'), may hold values from 0 to 1023, as said below
- col_index: int32 [64, 4, 2, 1024], P('blk', 'rep'), may hold values from 0 to 1023, as said below
Outputs:
- new_row_emb: bfloat16 [65536, 300], P('blk')
- new_col_emb: bfloat16 [65536, 300], P('blk')
Inputs may be any that keep to these rules, and one draw needn't show every extreme that they name: Every shard has some cell with count 1023, and zeros among its counts. `row_index`: each row of the last dimension lists every one of the 1024 positions once. `col_index`: each row of the last dimension lists every one of the 1024 positions once.
All inputs are finite; a program needn't handle non-finite values.
Results may differ from a plain program's by a relative error of at most 0.0031.
Values may be sent and summed in bfloat16 or wider, within the bound.
No kernel may reach another device: no remote copies, remote signals or barrier semaphores. Data moves between devices by JAX's collectives and lax.ppermute only.
A program may use at most 128 MiB of HBM per device.

v0:
```python
import jax
import jax.numpy as jnp
from jax import lax
from jax.experimental import pallas as pl
from jax.experimental.pallas import tpu as pltpu
from jax.sharding import PartitionSpec as P

LEARN_RATE = 0.05
DIM = 300
WIDE = 304
LOW = 160
HIGH = WIDE - LOW
FULL = DIM // 16 * 16
OFF = DIM
ONE = DIM + 1
DIGIT = 32
TERMS = 1024
CHUNK = 256
RING = 8
STRIDE = 8
AXES = ("blk", "rep")
F32 = jnp.float32
BF16 = jnp.bfloat16


def hop(name, array, moves):
    perm = []
    for blk in range(RING * STRIDE):
        for rep in range(4):
            if moves[rep] is None:
                continue
            by, to = moves[rep]
            dst = (blk + STRIDE * by) % (RING * STRIDE)
            perm.append((blk * 4 + rep, dst * 4 + to))
    with jax.named_scope(name):
        return lax.ppermute(array, AXES, perm)


CORE = [(0, 1), (0, 0), (0, 3), (0, 2)]
ACROSS = [(0, 2), (0, 3), (0, 0), (0, 1)]


def dot(a, b, ca, cb):
    return lax.dot_general(a, b, (((ca,), (cb,)), ((), ())), preferred_element_type=F32)


def one_hot(index):
    hit = lax.broadcasted_iota(jnp.int32, (TERMS, TERMS), 0) == index
    return jnp.where(hit, 1.0, 0.0).astype(BF16)


def shape(rows, dtype=BF16):
    return jax.ShapeDtypeStruct((rows, TERMS), dtype)


def vmem(rows, dtype=BF16):
    return pltpu.VMEM((rows, TERMS), dtype)


def cost(flops, moved, trans=0):
    return pl.CostEstimate(flops=flops, bytes_accessed=moved, transcendentals=trans)


MATMUL = 2 * WIDE * TERMS * TERMS


def last_rows(emb_ref, tail, rows):
    left = DIM - FULL
    tail[:left] = emb_ref[FULL:DIM].astype(F32)
    for i, row in enumerate(rows):
        tail[left + i : left + i + 1] = row
    return tail[...].astype(BF16)


def order(ref, swap):
    idx = ref[...].reshape(2, TERMS)
    one, two = idx[:1], idx[1:]
    return jnp.where(swap, two, one), jnp.where(swap, one, two)


def pack_kernel(swap_ref, emb_ref, off_ref, idx_ref, low_ref, high_ref, idx_out, tail):
    idx, idx_2 = order(idx_ref, swap_ref[0] == 1)
    idx_out[...] = idx_2
    zero = jnp.zeros((1, TERMS), F32)
    high = (idx // DIGIT).astype(F32)
    low = (idx % DIGIT).astype(F32)
    off = off_ref[...].astype(F32).reshape(1, TERMS)
    low_ref[...] = emb_ref[:LOW]
    high_ref[: FULL - LOW] = emb_ref[LOW:FULL]
    high_ref[FULL - LOW :] = last_rows(emb_ref, tail, [off, high, low, zero])


KERNEL_VMEM = 20 * 2**20
VMEM = pl.BlockSpec(memory_space=pltpu.VMEM)
SMEM = pl.BlockSpec(memory_space=pltpu.SMEM)
HBM = pl.BlockSpec(memory_space=pltpu.HBM)


def pack(swap, emb, off, idx):
    return pl.pallas_call(
        pack_kernel,
        out_shape=(shape(LOW), shape(HIGH), shape(1, jnp.int32)),
        in_specs=[SMEM] + [VMEM] * 3,
        out_specs=(VMEM,) * 3,
        scratch_shapes=[pltpu.VMEM((16, TERMS), F32)],
        cost_estimate=cost(0, 1300000),
    )(swap, emb, off, idx)


def rows_kernel(swap_ref, emb_ref, off_ref, idx_ref, row_1, row_2, wide, tail):
    zero = jnp.zeros((1, TERMS), F32)
    off = off_ref[...].astype(F32).reshape(1, TERMS)
    wide[:FULL] = emb_ref[:FULL]
    wide[FULL:] = last_rows(emb_ref, tail, [zero + 1.0, off, zero, zero])
    for idx, out in zip(order(idx_ref, swap_ref[0] == 1), (row_1, row_2)):
        out[...] = dot(wide[...], one_hot(idx), 1, 0).astype(BF16)


def pick_rows(swap, emb, off, idx):
    return pl.pallas_call(
        rows_kernel,
        out_shape=(shape(WIDE), shape(WIDE)),
        in_specs=[SMEM] + [VMEM] * 3,
        out_specs=(VMEM,) * 2,
        scratch_shapes=[pltpu.VMEM((WIDE, TERMS), BF16), pltpu.VMEM((16, TERMS), F32)],
        cost_estimate=cost(2 * MATMUL, 2000000),
    )(swap, emb, off, idx)


def weights(count):
    scale = 1.0 / TERMS
    count_f = count.astype(F32)
    slope = 0.1 * scale + (0.25 * scale) * (count_f * lax.rsqrt(count_f))
    base = slope * jnp.log(count_f)
    return jnp.where(count > 0, slope, 0.0), jnp.where(count > 0, base, 0.0)


def cells(score, slope, base):
    scale = 0.5 / TERMS
    unseen = scale + scale * jnp.tanh(0.5 * score)
    return jnp.where(slope > 0, slope * score - base, unseen).astype(BF16)


CHUNKS = [slice(i, i + CHUNK) for i in range(0, TERMS, CHUNK)]


def fetch(pairs, sems):
    copies = [
        pltpu.make_async_copy(src, dst, sems.at[i]) for i, (src, dst) in enumerate(pairs)
    ]
    for copy in copies:
        copy.start()
    return copies


def pick_cols(block, pick):
    col = dot(block, pick, 1, 0)
    row = lax.broadcasted_iota(jnp.int32, (WIDE, TERMS), 0)
    return jnp.where(row > OFF, jnp.where(row == ONE, 1.0, 0.0), col).astype(BF16)


def put_halves(value, low_out, high_out):
    low_out[...] = value[:LOW]
    high_out[:HIGH] = value[LOW:]
    high_out[HIGH:] = jnp.zeros((LOW - HIGH, TERMS), BF16)


def first_kernel(
    swap_ref, counts_ref, row_ref, row_idx_ref, low_ref, high_ref, low_out, high_out, row_out,
    counts, cell_buf, row, sems,
):
    swap = swap_ref[0]
    at = [pl.ds(part.start, CHUNK) for part in CHUNKS]
    copies = fetch(
        [(row_ref, row)] + [(counts_ref.at[swap, part], counts.at[part]) for part in at], sems
    )
    digits = high_ref[HIGH - 16 :].astype(F32)
    one = ONE - (WIDE - 16)
    idx = (digits[one : one + 1] * DIGIT + digits[one + 1 : one + 2]).astype(jnp.int32)
    pick = one_hot(idx)
    col = pick_cols(jnp.concatenate([low_ref[...], high_ref[...]], axis=0), pick)
    copies[0].wait()
    for copy, part in zip(copies[1:], CHUNKS):
        score = dot(row[:, part], col, 0, 0)
        copy.wait()
        cell_buf[part] = cells(score, *weights(counts[part]))
    grad = dot(row[...], cell_buf[...], 1, 0).astype(BF16)
    put_halves(dot(grad, pick, 1, 1).astype(BF16), low_out, high_out)
    row_pick = one_hot(order(row_idx_ref, swap == 1)[0])
    row_out[...] = dot(dot(col, cell_buf[...], 1, 1).astype(BF16), row_pick, 1, 1)


def first_pair(swap, *args):
    return pl.pallas_call(
        first_kernel,
        out_shape=(shape(LOW), shape(LOW), shape(WIDE, F32)),
        in_specs=[SMEM, HBM, HBM] + [VMEM] * 3,
        out_specs=(VMEM,) * 3,
        scratch_shapes=[
            pltpu.VMEM((TERMS, TERMS), jnp.int32),
            pltpu.VMEM((TERMS, TERMS), BF16),
            pltpu.VMEM((WIDE, TERMS), BF16),
            pltpu.SemaphoreType.DMA((1 + len(CHUNKS),)),
        ],
        compiler_params=pltpu.CompilerParams(vmem_limit_bytes=KERNEL_VMEM),
        cost_estimate=cost(6 * MATMUL, 12000000, 3 * TERMS * TERMS),
    )(swap, *args)


def weigh_kernel(swap_ref, counts_ref, out_ref, buf, sems):
    at = [pl.ds(part.start, CHUNK) for part in CHUNKS]
    copies = fetch([(counts_ref.at[1 - swap_ref[0], part], buf.at[part]) for part in at], sems)
    for copy, part in zip(copies, CHUNKS):
        copy.wait()
        slope, base = weights(buf[part])
        out_ref[0, part] = slope.astype(BF16)
        out_ref[1, part] = base.astype(BF16)


def weigh(swap, counts):
    return pl.pallas_call(
        weigh_kernel,
        out_shape=jax.ShapeDtypeStruct((2, TERMS, TERMS), BF16),
        in_specs=[SMEM, HBM],
        out_specs=VMEM,
        scratch_shapes=[
            pltpu.VMEM((TERMS, TERMS), jnp.int32),
            pltpu.SemaphoreType.DMA((len(CHUNKS),)),
        ],
        compiler_params=pltpu.CompilerParams(vmem_limit_bytes=KERNEL_VMEM),
        cost_estimate=cost(20 * TERMS * TERMS, 8000000, 4 * TERMS * TERMS),
    )(swap, counts)


def second_kernel(
    swap_ref, weights_ref, row_ref, prev_ref, row_idx_ref, idx_ref, low_ref, high_ref, low_2_ref,
    high_2_ref, low_out, high_out, row_low_out, row_high_out, weight, cell_buf, row, prev, sems,
):
    at = [pl.ds(part.start, CHUNK) for part in CHUNKS]
    copies = fetch(
        [(row_ref, row)]
        + [(weights_ref.at[:, part], weight.at[:, part]) for part in at]
        + [(prev_ref, prev)],
        sems,
    )
    low = low_ref[...] + low_2_ref[...]
    high = high_ref[...] + high_2_ref[...]
    pick = one_hot(idx_ref[...])
    col = pick_cols(jnp.concatenate([low, high], axis=0), pick)
    copies[0].wait()
    for copy, part in zip(copies[1:-1], CHUNKS):
        score = dot(row[:, part], col, 0, 0)
        copy.wait()
        slope, base = weight[0, part].astype(F32), weight[1, part].astype(F32)
        cell_buf[part] = cells(score, slope, base)
    grad = dot(row[...], cell_buf[...], 1, 0).astype(BF16)
    put_halves(dot(grad, pick, 1, 1).astype(BF16), low_out, high_out)
    row_pick = one_hot(order(row_idx_ref, swap_ref[0] == 1)[1])
    total = dot(dot(col, cell_buf[...], 1, 1).astype(BF16), row_pick, 1, 1)
    copies[-1].wait()
    put_halves((prev[...] + total).astype(BF16), row_low_out, row_high_out)


def second_pair(swap, *args):
    return pl.pallas_call(
        second_kernel,
        out_shape=(vmem(LOW), vmem(LOW), shape(LOW), shape(LOW)),
        in_specs=[SMEM] + [HBM] * 3 + [VMEM] * 6,
        out_specs=(VMEM,) * 4,
        scratch_shapes=[
            pltpu.VMEM((2, TERMS, TERMS), BF16),
            pltpu.VMEM((TERMS, TERMS), BF16),
            pltpu.VMEM((WIDE, TERMS), BF16),
            pltpu.VMEM((WIDE, TERMS), F32),
            pltpu.SemaphoreType.DMA((2 + len(CHUNKS),)),
        ],
        compiler_params=pltpu.CompilerParams(vmem_limit_bytes=KERNEL_VMEM),
        cost_estimate=cost(6 * MATMUL, 12000000, TERMS * TERMS),
    )(swap, *args)


def adagrad(core, mine, other, table, acc):
    low = jnp.where(core == 0, mine, other)
    high = jnp.where(core == 0, other, mine)[: DIM - LOW]
    total = jnp.concatenate([low, high]).astype(F32)
    step = LEARN_RATE * total * lax.rsqrt(acc + total * total)
    return (table.astype(F32) - step).astype(BF16)


def in_hbm(array):
    return pltpu.with_memory_space_constraint(array, pltpu.HBM)


def add(*parts):
    total = parts[0].astype(F32)
    for part in parts[1:]:
        total = total + part.astype(F32)
    return total.astype(BF16)


def per_device(
    row_emb, col_emb, row_acc, col_acc, row_offset, col_offset, counts, row_index, col_index
):
    replica = lax.axis_index("rep")
    core = replica & 1
    is_0, is_1, is_3 = replica == 0, replica == 1, replica == 3
    swap = is_3.astype(jnp.int32).reshape(1)
    counts = in_hbm(counts.reshape(counts.shape[2:]))

    barrier = lax.optimization_barrier
    low, high, col_idx_2 = pack(swap, col_emb.T, col_offset, col_index)
    got_low = hop("got_low", low, [(0, 0), (-1, 1), (-2, 2), (1, 3)])
    far = hop("far", low, [None, (3, 1), None, None])
    got_high = hop("got_high", high, [(0, 0), (-1, 1), (-2, 2), (1, 3)])
    idx_2 = hop("idx_2", col_idx_2, [(-4, 0), (3, 1), (2, 2), (-3, 3)])
    row_1, row_2 = pick_rows(swap, row_emb.T, row_offset, row_index)
    weights_2 = weigh(swap, counts)
    got_low, got_high, far, idx_2, row_1, weights_2 = barrier(
        (got_low, got_high, far, idx_2, row_1, weights_2)
    )
    high_2 = hop("high_2", got_high, [None, (-3, 0), (-1, 3), (1, 2)])
    low_2 = hop("low_2", jnp.where(is_1, far, got_low), [None, (1, 0), (-1, 3), (1, 2)])
    low_1, high_1, row_sum = first_pair(
        swap, counts, in_hbm(row_1), row_index, got_low, got_high
    )
    high_2, low_2, low_1 = barrier((high_2, low_2, low_1))
    high_far = hop("high_far", high_2, [(-1, 1), None, None, None])
    give_low, give_high, row_low, row_high = second_pair(
        swap, in_hbm(weights_2), in_hbm(row_2), in_hbm(row_sum),
        row_index, idx_2, far, high_far, low_2, high_2,
    )

    s_low = hop("s_low", give_low, [(-1, 1), None, (-1, 3), (1, 2)])
    s_high = jnp.where(is_0, high_1, give_high)
    s_high = hop("s_high", s_high, [(0, 1), (1, 0), (-1, 3), (1, 2)])
    keep = jnp.where(core == 0, row_low, row_high)
    give = jnp.where(core == 0, row_high, row_low)
    row_chip = add(keep, hop("row_swap", give, CORE))
    s_low, s_high, row_chip = barrier((s_low, s_high, row_chip))
    one = jnp.where(is_0, give_high, jnp.where(is_1, give_low, jnp.where(is_3, high_1, low_1)))
    one = add(one, jnp.where(is_0 | is_3, s_high, s_low))
    one = hop("one", one, [(3, 1), (-3, 0), (2, 2), (-1, 3)])
    two = jnp.where(replica == 2, add(high_1, s_high), add(low_1, jnp.where(is_3, s_low, 0)))
    two = hop("two", two, [None, (1, 0), (2, 3), (-1, 2)])
    row_across = hop("row_across", row_chip, ACROSS)
    one, two = barrier((one, two))
    last = hop("last", add(high_1, one), [None, (1, 1), None, None])

    row_mine = add(row_chip, row_across)
    row_other = hop("row_other", row_mine, CORE)
    col_chip = add(
        jnp.where(is_1, s_high, one),
        jnp.where(is_1, last, two),
        jnp.where(is_0, low_1, 0),
    )
    col_across = hop("col_across", col_chip, ACROSS)
    new_row = adagrad(core, row_mine, row_other, row_emb.T, row_acc.T)
    col_across, new_row = barrier((col_across, new_row))
    col_mine = add(col_chip, col_across)
    col_other = hop("col_other", col_mine, CORE)
    new_col = adagrad(core, col_mine, col_other, col_emb.T, col_acc.T)
    return (new_row.T, new_col.T)


def solution(mesh):
    in_specs = (
        P("blk", None),
        P("blk", None),
        P("blk", None),
        P("blk", None),
        P("blk"),
        P("blk"),
        P("blk", "rep", None, None, None),
        P("blk", "rep", None, None),
        P("blk", "rep", None, None),
    )
    out_specs = (P("blk", None), P("blk", None))
    return jax.shard_map(
        per_device, mesh=mesh, in_specs=in_specs, out_specs=out_specs, check_vma=False
    )
```

profile of v0, /device:TPU:1, one launch (start us, length us, event | category | flops | bytes accessed | tf_op | source)
XLA Modules:
  0.0 106.8 jit_solution(16293425328402433500)
XLA Ops:
  0.6 2.0 %shard_map.104 = (bf16[160,1024]{1,0:T(8,128)(2,1)}, bf16[144,1024]{1,0:T(8,128)(2,1)}, s32[1,1024]{1,0:T(1,128)}) custom-call(s32[1]{0:T(128)} %bitcast.swap_ref, bf16[300,1024]{1,0:T(8,128)(2,1)} %bitcast.17, bf16[1024]{0:T(1024)(128)(2,1)} %off_ref.2, s32[1,1,2,1024]{3,2,1,0:T(2,128)} %idx_ref.2), custom_call_target="tpu_custom_call" | custom-call | bytes 1300000 | tf_op jit(solution)/shard_map/pallas_call | solution.py:100
  2.6 8.3 %collective-permute-start = (bf16[160,1024]{1,0:T(8,128)(2,1)}, bf16[160,1024]{1,0:T(8,128)(2,1)S(1)}, u32[]{:S(2)}, u32[]{:S(2)}) collective-permute-start(bf16[160,1024]{1,0:T(8,128)(2,1)} %get-tuple-element.30), channel_id=1, source_target_pairs={{0,0},{1,225},{2,194},{3,35},{4,4},{5,229},{6,198},{7,39},{8,8},{9... | collective-permute-start | bytes 983048 | tf_op jit(solution)/shard_map/got_low/ppermute | solution.py:36
  10.9 1.9 %collective-permute-start.2 = (bf16[160,1024]{1,0:T(8,128)(2,1)}, bf16[160,1024]{1,0:T(8,128)(2,1)S(1)}, u32[]{:S(2)}, u32[]{:S(2)}) collective-permute-start(bf16[160,1024]{1,0:T(8,128)(2,1)} %get-tuple-element.30), channel_id=1, source_target_pairs={{1,97},{5,101},{9,105},{13,109},{17,113},{21,117},{25,121},{29,125... | collective-permute-start | bytes 983048 | tf_op jit(solution)/shard_map/far/ppermute | solution.py:36
  12.9 2.6 %collective-permute-start.1 = (bf16[144,1024]{1,0:T(8,128)(2,1)}, bf16[144,1024]{1,0:T(8,128)(2,1)S(1)}, u32[]{:S(2)}, u32[]{:S(2)}) collective-permute-start(bf16[144,1024]{1,0:T(8,128)(2,1)} %get-tuple-element.31), channel_id=1, source_target_pairs={{0,0},{1,225},{2,194},{3,35},{4,4},{5,229},{6,198},{7,39},{8,8},{9... | collective-permute-start | bytes 884744 | tf_op jit(solution)/shard_map/got_high/ppermute | solution.py:36
  15.5 3.3 %collective-permute-start.3 = (s32[1,1024]{1,0:T(1,128)}, s32[1,1024]{1,0:T(1,128)S(1)}, u32[]{:S(2)}, u32[]{:S(2)}) collective-permute-start(s32[1,1024]{1,0:T(1,128)} %get-tuple-element.32), channel_id=1, source_target_pairs={{0,128},{1,97},{2,66},{3,163},{4,132},{5,101},{6,70},{7,167},{8,13... | collective-permute-start | bytes 12296 | tf_op jit(solution)/shard_map/idx_2/ppermute | solution.py:36
  18.8 3.4 %shard_map.105 = (bf16[304,1024]{1,0:T(8,128)(2,1)}, bf16[304,1024]{1,0:T(8,128)(2,1)}) custom-call(s32[1]{0:T(128)} %bitcast.swap_ref, bf16[300,1024]{1,0:T(8,128)(2,1)} %bitcast.18, bf16[1024]{0:T(1024)(128)(2,1)} %off_ref.3, s32[1,1,2,1024]{3,2,1,0:T(2,128)} %row_idx_ref.3), custom_call_target="tpu_custom_call" | custom-call | flops 1275068416 | bytes 2000000 | tf_op jit(solution)/shard_map/pallas_call | solution.py:120
  22.2 3.2 %shard_map.106.weights_ref = bf16[2,1024,1024]{2,1,0:T(8,128)(2,1)S(1)} custom-call(s32[1]{0:T(128)} %bitcast.swap_ref, s32[2,1024,1024]{2,1,0:T(8,128)} %bitcast.15), custom_call_target="tpu_custom_call" | custom-call | flops 20971520 | bytes 8000000 | tf_op jit(solution)/shard_map/pallas_call | solution.py:221
  25.4 1.9 %copy-done = bf16[2,1024,1024]{2,1,0:T(8,128)(2,1)} copy-done((bf16[2,1024,1024]{2,1,0:T(8,128)(2,1)}, bf16[2,1024,1024]{2,1,0:T(8,128)(2,1)S(1)}, u32[]{:S(2)}) %copy-start) | copy-done | bytes 4194328
  28.8 1.5 %collective-permute-start.5 = (bf16[160,1024]{1,0:T(8,128)(2,1)S(1)}, bf16[160,1024]{1,0:T(8,128)(2,1)S(1)}, u32[]{:S(2)}, u32[]{:S(2)}) collective-permute-start(bf16[160,1024]{1,0:T(8,128)(2,1)S(1)} %broadcast_select_fusion.4), channel_id=1, source_target_pairs={{1,32},{2,227},{3,34},{5,36},{6,231},{7,38},{9,40},{10,235},{11,42... | collective-permute-start | bytes 983048 | tf_op jit(solution)/shard_map/low_2/ppermute | solution.py:36
  30.3 9.9 %shard_map.107 = (bf16[160,1024]{1,0:T(8,128)(2,1)S(1)}, bf16[160,1024]{1,0:T(8,128)(2,1)S(1)}, f32[304,1024]{1,0:T(8,128)S(1)}) custom-call(s32[1]{0:T(128)} %bitcast.swap_ref, s32[2,1024,1024]{2,1,0:T(8,128)} %bitcast.16, bf16[304,1024]{1,0:T(8,128)(2,1)} %get-tuple-element.36.row_ref, s32[1,1,2,1024]{3,2,1,0:T(2,128)S(1)} %copy-done.1, ...), custom_call_target="tpu_custom_call" | custom-call | flops 3825205248 | bytes 12000000 | tf_op jit(solution)/shard_map/pallas_call | solution.py:194
  41.3 1.5 %collective-permute-start.6 = (bf16[144,1024]{1,0:T(8,128)(2,1)S(1)}, bf16[144,1024]{1,0:T(8,128)(2,1)S(1)}, u32[]{:S(2)}, u32[]{:S(2)}) collective-permute-start(bf16[144,1024]{1,0:T(8,128)(2,1)S(1)} %collective-permute-done.4.high_2_ref), channel_id=1, source_target_pairs={{0,225},{4,229},{8,233},{12,237},{16,241},{20,245},{24,249},{28,25... | collective-permute-start | bytes 884744 | tf_op jit(solution)/shard_map/high_far/ppermute | solution.py:36
  42.8 6.5 %collective-permute-done.6.high_ref = bf16[144,1024]{1,0:T(8,128)(2,1)S(1)} collective-permute-done((bf16[144,1024]{1,0:T(8,128)(2,1)S(1)}, bf16[144,1024]{1,0:T(8,128)(2,1)S(1)}, u32[]{:S(2)}, u32[]{:S(2)}) %collective-permute-start.6) | collective-permute-done | bytes 294944 | tf_op jit(solution)/shard_map/high_far/ppermute | solution.py:36
  49.3 8.0 %shard_map.108 = (bf16[160,1024]{1,0:T(8,128)(2,1)S(1)}, bf16[160,1024]{1,0:T(8,128)(2,1)S(1)}, bf16[160,1024]{1,0:T(8,128)(2,1)S(1)}, bf16[160,1024]{1,0:T(8,128)(2,1)S(1)}) custom-call(s32[1]{0:T(128)} %bitcast.swap_ref, bf16[2,1024,1024]{2,1,0:T(8,128)(2,1)} %copy-done, bf16[304,1024]{1,0:T(8,128)(2,1)} %get-tuple-element.35.row_ref, ...), custom_call_target="tpu_custom_call" | custom-call | flops 3825205248 | bytes 12000000 | tf_op jit(solution)/shard_map/pallas_call | solution.py:265
  58.9 2.5 %collective-permute-start.8 = (bf16[160,1024]{1,0:T(8,128)(2,1)S(1)}, bf16[160,1024]{1,0:T(8,128)(2,1)S(1)}, u32[]{:S(2)}, u32[]{:S(2)}) collective-permute-start(bf16[160,1024]{1,0:T(8,128)(2,1)S(1)} %broadcast_select_fusion.3), channel_id=1, source_target_pairs={{0,1},{1,32},{2,227},{3,34},{4,5},{5,36},{6,231},{7,38},{8,9},{9,4... | collective-permute-start | bytes 983048 | tf_op jit(solution)/shard_map/s_high/ppermute | solution.py:36
  62.5 3.4 %collective-permute-done.7 = bf16[160,1024]{1,0:T(8,128)(2,1)S(1)} collective-permute-done((bf16[160,1024]{1,0:T(8,128)(2,1)S(1)}, bf16[160,1024]{1,0:T(8,128)(2,1)S(1)}, u32[]{:S(2)}, u32[]{:S(2)}) %collective-permute-start.7) | collective-permute-done | bytes 327712 | tf_op jit(solution)/shard_map/s_low/ppermute | solution.py:36
  66.0 4.5 %collective-permute-start.10 = (bf16[160,1024]{1,0:T(8,128)(2,1)S(1)}, bf16[160,1024]{1,0:T(8,128)(2,1)S(1)}, u32[]{:S(2)}, u32[]{:S(2)}) collective-permute-start(bf16[160,1024]{1,0:T(8,128)(2,1)S(1)} %add_convert_fusion.4), channel_id=1, source_target_pairs={{0,97},{1,160},{2,66},{3,227},{4,101},{5,164},{6,70},{7,231},{8,10... | collective-permute-start | bytes 983048 | tf_op jit(solution)/shard_map/one/ppermute | solution.py:36
  70.8 1.7 %collective-permute-start.11 = (bf16[160,1024]{1,0:T(8,128)(2,1)S(1)}, bf16[160,1024]{1,0:T(8,128)(2,1)S(1)}, u32[]{:S(2)}, u32[]{:S(2)}) collective-permute-start(bf16[160,1024]{1,0:T(8,128)(2,1)S(1)} %fusion.13), channel_id=1, source_target_pairs={{1,32},{2,67},{3,226},{5,36},{6,71},{7,230},{9,40},{10,75},{11,234... | collective-permute-start | bytes 983048 | tf_op jit(solution)/shard_map/two/ppermute | solution.py:36
  72.6 1.7 %collective-permute-start.14 = (bf16[160,1024]{1,0:T(8,128)(2,1)S(1)}, bf16[160,1024]{1,0:T(8,128)(2,1)S(1)}, u32[]{:S(2)}, u32[]{:S(2)}) collective-permute-start(bf16[160,1024]{1,0:T(8,128)(2,1)S(1)} %add_convert_fusion.5), channel_id=1, source_target_pairs={{0,2},{1,3},{2,0},{3,1},{4,6},{5,7},{6,4},{7,5},{8,10},{9,11},{10,... | collective-permute-start | bytes 983048 | tf_op jit(solution)/shard_map/row_across/ppermute | solution.py:36
  74.3 4.1 %collective-permute-done.10 = bf16[160,1024]{1,0:T(8,128)(2,1)S(1)} collective-permute-done((bf16[160,1024]{1,0:T(8,128)(2,1)S(1)}, bf16[160,1024]{1,0:T(8,128)(2,1)S(1)}, u32[]{:S(2)}, u32[]{:S(2)}) %collective-permute-start.10) | collective-permute-done | bytes 327712 | tf_op jit(solution)/shard_map/one/ppermute | solution.py:36
  78.4 8.0 %collective-permute-done.11 = bf16[160,1024]{1,0:T(8,128)(2,1)S(1)} collective-permute-done((bf16[160,1024]{1,0:T(8,128)(2,1)S(1)}, bf16[160,1024]{1,0:T(8,128)(2,1)S(1)}, u32[]{:S(2)}, u32[]{:S(2)}) %collective-permute-start.11) | collective-permute-done | bytes 327712 | tf_op jit(solution)/shard_map/two/ppermute | solution.py:36
  86.5 1.9 %collective-permute-start.12 = (bf16[160,1024]{1,0:T(8,128)(2,1)S(1)}, bf16[160,1024]{1,0:T(8,128)(2,1)S(1)}, u32[]{:S(2)}, u32[]{:S(2)}) collective-permute-start(bf16[160,1024]{1,0:T(8,128)(2,1)S(1)} %fusion.11), channel_id=1, source_target_pairs={{1,33},{5,37},{9,41},{13,45},{17,49},{21,53},{25,57},{29,61},{33,6... | collective-permute-start | bytes 983048 | tf_op jit(solution)/shard_map/last/ppermute | solution.py:36
  88.7 7.2 %collective-permute-done.12 = bf16[160,1024]{1,0:T(8,128)(2,1)S(1)} collective-permute-done((bf16[160,1024]{1,0:T(8,128)(2,1)S(1)}, bf16[160,1024]{1,0:T(8,128)(2,1)S(1)}, u32[]{:S(2)}, u32[]{:S(2)}) %collective-permute-start.12) | collective-permute-done | bytes 327712 | tf_op jit(solution)/shard_map/last/ppermute | solution.py:36
  98.8 4.9 %collective-permute-done.13 = bf16[160,1024]{1,0:T(8,128)(2,1)S(1)} collective-permute-done((bf16[160,1024]{1,0:T(8,128)(2,1)S(1)}, bf16[160,1024]{1,0:T(8,128)(2,1)S(1)}, u32[]{:S(2)}, u32[]{:S(2)}) %collective-permute-start.13) | collective-permute-done | bytes 327712 | tf_op jit(solution)/shard_map/col_across/ppermute | solution.py:36
  103.9 1.6 %collective-permute-done.16 = bf16[160,1024]{1,0:T(8,128)(2,1)S(1)} collective-permute-done((bf16[160,1024]{1,0:T(8,128)(2,1)S(1)}, bf16[160,1024]{1,0:T(8,128)(2,1)S(1)}, u32[]{:S(2)}, u32[]{:S(2)}) %collective-permute-start.16) | collective-permute-done | bytes 327712 | tf_op jit(solution)/shard_map/col_other/ppermute | solution.py:36
  (45 shorter events, 10.0 us)
Async XLA Ops:
  2.6 24.8 %collective-permute-start = (bf16[160,1024]{1,0:T(8,128)(2,1)}, bf16[160,1024]{1,0:T(8,128)(2,1)S(1)}, u32[]{:S(2)}, u32[]{:S(2)}) collective-permute-start(bf16[160,1024]{1,0:T(8,128)(2,1)} %get-tuple-element.30), channel_id=1, source_target_pairs={{0,0},{1,225},{2,194},{3,35},{4,4},{5,229},{6,198},{7,39},{8,8},{9... | collective-permute-start | bytes 983048 | tf_op jit(solution)/shard_map/got_low/ppermute | solution.py:36
  10.9 16.5 %collective-permute-start.2 = (bf16[160,1024]{1,0:T(8,128)(2,1)}, bf16[160,1024]{1,0:T(8,128)(2,1)S(1)}, u32[]{:S(2)}, u32[]{:S(2)}) collective-permute-start(bf16[160,1024]{1,0:T(8,128)(2,1)} %get-tuple-element.30), channel_id=1, source_target_pairs={{1,97},{5,101},{9,105},{13,109},{17,113},{21,117},{25,121},{29,125... | collective-permute-start | bytes 983048 | tf_op jit(solution)/shard_map/far/ppermute | solution.py:36
  12.9 14.5 %collective-permute-start.1 = (bf16[144,1024]{1,0:T(8,128)(2,1)}, bf16[144,1024]{1,0:T(8,128)(2,1)S(1)}, u32[]{:S(2)}, u32[]{:S(2)}) collective-permute-start(bf16[144,1024]{1,0:T(8,128)(2,1)} %get-tuple-element.31), channel_id=1, source_target_pairs={{0,0},{1,225},{2,194},{3,35},{4,4},{5,229},{6,198},{7,39},{8,8},{9... | collective-permute-start | bytes 884744 | tf_op jit(solution)/shard_map/got_high/ppermute | solution.py:36
  15.5 11.9 %collective-permute-start.3 = (s32[1,1024]{1,0:T(1,128)}, s32[1,1024]{1,0:T(1,128)S(1)}, u32[]{:S(2)}, u32[]{:S(2)}) collective-permute-start(s32[1,1024]{1,0:T(1,128)} %get-tuple-element.32), channel_id=1, source_target_pairs={{0,128},{1,97},{2,66},{3,163},{4,132},{5,101},{6,70},{7,167},{8,13... | collective-permute-start | bytes 12296 | tf_op jit(solution)/shard_map/idx_2/ppermute | solution.py:36
  22.2 8.0 %copy-start.1 = (s32[1,1,2,1024]{3,2,1,0:T(2,128)S(1)}, s32[1,1,2,1024]{3,2,1,0:T(2,128)}, u32[]{:S(2)}) copy-start(s32[1,1,2,1024]{3,2,1,0:T(2,128)} %row_idx_ref.3) | copy-start | bytes 24580
  25.4 2.0 %copy-start = (bf16[2,1024,1024]{2,1,0:T(8,128)(2,1)}, bf16[2,1024,1024]{2,1,0:T(8,128)(2,1)S(1)}, u32[]{:S(2)}) copy-start(bf16[2,1024,1024]{2,1,0:T(8,128)(2,1)S(1)} %shard_map.106.weights_ref) | copy-start | bytes 12582916
  27.4 13.9 %collective-permute-start.4 = (bf16[144,1024]{1,0:T(8,128)(2,1)S(1)}, bf16[144,1024]{1,0:T(8,128)(2,1)S(1)}, u32[]{:S(2)}, u32[]{:S(2)}) collective-permute-start(bf16[144,1024]{1,0:T(8,128)(2,1)S(1)} %collective-permute-done.1.high_ref), channel_id=1, source_target_pairs={{1,160},{2,227},{3,34},{5,164},{6,231},{7,38},{9,168},{10,235},{11... | collective-permute-start | bytes 884744 | tf_op jit(solution)/shard_map/high_2/ppermute | solution.py:36
  28.8 12.5 %collective-permute-start.5 = (bf16[160,1024]{1,0:T(8,128)(2,1)S(1)}, bf16[160,1024]{1,0:T(8,128)(2,1)S(1)}, u32[]{:S(2)}, u32[]{:S(2)}) collective-permute-start(bf16[160,1024]{1,0:T(8,128)(2,1)S(1)} %broadcast_select_fusion.4), channel_id=1, source_target_pairs={{1,32},{2,227},{3,34},{5,36},{6,231},{7,38},{9,40},{10,235},{11,42... | collective-permute-start | bytes 983048 | tf_op jit(solution)/shard_map/low_2/ppermute | solution.py:36
  40.2 1.1 %copy-start.2 = (f32[304,1024]{1,0:T(8,128)}, f32[304,1024]{1,0:T(8,128)S(1)}, u32[]{:S(2)}) copy-start(f32[304,1024]{1,0:T(8,128)S(1)} %get-tuple-element.39.prev_ref) | copy-start | bytes 3735556
  41.3 8.0 %collective-permute-start.6 = (bf16[144,1024]{1,0:T(8,128)(2,1)S(1)}, bf16[144,1024]{1,0:T(8,128)(2,1)S(1)}, u32[]{:S(2)}, u32[]{:S(2)}) collective-permute-start(bf16[144,1024]{1,0:T(8,128)(2,1)S(1)} %collective-permute-done.4.high_2_ref), channel_id=1, source_target_pairs={{0,225},{4,229},{8,233},{12,237},{16,241},{20,245},{24,249},{28,25... | collective-permute-start | bytes 884744 | tf_op jit(solution)/shard_map/high_far/ppermute | solution.py:36
  57.4 3.9 %collective-permute-start.9 = (bf16[160,1024]{1,0:T(8,128)(2,1)S(1)}, bf16[160,1024]{1,0:T(8,128)(2,1)}, u32[]{:S(2)}, u32[]{:S(2)}) collective-permute-start(bf16[160,1024]{1,0:T(8,128)(2,1)S(1)} %broadcast_select_fusion.2), channel_id=1, source_target_pairs={{0,1},{1,0},{2,3},{3,2},{4,5},{5,4},{6,7},{7,6},{8,9},{9,8},{10,11... | collective-permute-start | bytes 983048 | tf_op jit(solution)/shard_map/row_swap/ppermute | solution.py:36
  57.5 8.4 %collective-permute-start.7 = (bf16[160,1024]{1,0:T(8,128)(2,1)S(1)}, bf16[160,1024]{1,0:T(8,128)(2,1)S(1)}, u32[]{:S(2)}, u32[]{:S(2)}) collective-permute-start(bf16[160,1024]{1,0:T(8,128)(2,1)S(1)} %get-tuple-element.45), channel_id=1, source_target_pairs={{0,225},{2,227},{3,34},{4,229},{6,231},{7,38},{8,233},{10,235},{11... | collective-permute-start | bytes 983048 | tf_op jit(solution)/shard_map/s_low/ppermute | solution.py:36
  58.9 7.1 %collective-permute-start.8 = (bf16[160,1024]{1,0:T(8,128)(2,1)S(1)}, bf16[160,1024]{1,0:T(8,128)(2,1)S(1)}, u32[]{:S(2)}, u32[]{:S(2)}) collective-permute-start(bf16[160,1024]{1,0:T(8,128)(2,1)S(1)} %broadcast_select_fusion.3), channel_id=1, source_target_pairs={{0,1},{1,32},{2,227},{3,34},{4,5},{5,36},{6,231},{7,38},{8,9},{9,4... | collective-permute-start | bytes 983048 | tf_op jit(solution)/shard_map/s_high/ppermute | solution.py:36
  66.0 12.4 %collective-permute-start.10 = (bf16[160,1024]{1,0:T(8,128)(2,1)S(1)}, bf16[160,1024]{1,0:T(8,128)(2,1)S(1)}, u32[]{:S(2)}, u32[]{:S(2)}) collective-permute-start(bf16[160,1024]{1,0:T(8,128)(2,1)S(1)} %add_convert_fusion.4), channel_id=1, source_target_pairs={{0,97},{1,160},{2,66},{3,227},{4,101},{5,164},{6,70},{7,231},{8,10... | collective-permute-start | bytes 983048 | tf_op jit(solution)/shard_map/one/ppermute | solution.py:36
  70.8 15.6 %collective-permute-start.11 = (bf16[160,1024]{1,0:T(8,128)(2,1)S(1)}, bf16[160,1024]{1,0:T(8,128)(2,1)S(1)}, u32[]{:S(2)}, u32[]{:S(2)}) collective-permute-start(bf16[160,1024]{1,0:T(8,128)(2,1)S(1)} %fusion.13), channel_id=1, source_target_pairs={{1,32},{2,67},{3,226},{5,36},{6,71},{7,230},{9,40},{10,75},{11,234... | collective-permute-start | bytes 983048 | tf_op jit(solution)/shard_map/two/ppermute | solution.py:36
  72.6 15.9 %collective-permute-start.14 = (bf16[160,1024]{1,0:T(8,128)(2,1)S(1)}, bf16[160,1024]{1,0:T(8,128)(2,1)S(1)}, u32[]{:S(2)}, u32[]{:S(2)}) collective-permute-start(bf16[160,1024]{1,0:T(8,128)(2,1)S(1)} %add_convert_fusion.5), channel_id=1, source_target_pairs={{0,2},{1,3},{2,0},{3,1},{4,6},{5,7},{6,4},{7,5},{8,10},{9,11},{10,... | collective-permute-start | bytes 983048 | tf_op jit(solution)/shard_map/row_across/ppermute | solution.py:36
  86.5 9.3 %collective-permute-start.12 = (bf16[160,1024]{1,0:T(8,128)(2,1)S(1)}, bf16[160,1024]{1,0:T(8,128)(2,1)S(1)}, u32[]{:S(2)}, u32[]{:S(2)}) collective-permute-start(bf16[160,1024]{1,0:T(8,128)(2,1)S(1)} %fusion.11), channel_id=1, source_target_pairs={{1,33},{5,37},{9,41},{13,45},{17,49},{21,53},{25,57},{29,61},{33,6... | collective-permute-start | bytes 983048 | tf_op jit(solution)/shard_map/last/ppermute | solution.py:36
  88.6 7.7 %collective-permute-start.15 = (bf16[160,1024]{1,0:T(8,128)(2,1)S(1)}, bf16[160,1024]{1,0:T(8,128)(2,1)S(1)}, u32[]{:S(2)}, u32[]{:S(2)}) collective-permute-start(bf16[160,1024]{1,0:T(8,128)(2,1)S(1)} %add_convert_fusion.1), channel_id=1, source_target_pairs={{0,1},{1,0},{2,3},{3,2},{4,5},{5,4},{6,7},{7,6},{8,9},{9,8},{10,11... | collective-permute-start | bytes 983048 | tf_op jit(solution)/shard_map/row_other/ppermute | solution.py:36
  96.1 1.3 %copy-start.4 = (f32[1024,300]{0,1:T(8,128)S(1)}, f32[1024,300]{0,1:T(8,128)}, u32[]{:S(2)}) copy-start(f32[1024,300]{0,1:T(8,128)} %param.11) | copy-start | bytes 3686404
  96.2 1.4 %copy-start.6 = (bf16[1024,300]{0,1:T(8,128)(2,1)S(1)}, bf16[1024,300]{0,1:T(8,128)(2,1)}, u32[]{:S(2)}) copy-start(bf16[1024,300]{0,1:T(8,128)(2,1)} %param.9) | copy-start | bytes 1843204
  96.2 7.5 %collective-permute-start.13 = (bf16[160,1024]{1,0:T(8,128)(2,1)S(1)}, bf16[160,1024]{1,0:T(8,128)(2,1)S(1)}, u32[]{:S(2)}, u32[]{:S(2)}) collective-permute-start(bf16[160,1024]{1,0:T(8,128)(2,1)S(1)} %add_convert_fusion.2), channel_id=1, source_target_pairs={{0,2},{1,3},{2,0},{3,1},{4,6},{5,7},{6,4},{7,5},{8,10},{9,11},{10,... | collective-permute-start | bytes 983048 | tf_op jit(solution)/shard_map/col_across/ppermute | solution.py:36
  98.8 6.8 %copy-start.3 = (bf16[1024,300]{0,1:T(8,128)(2,1)S(1)}, bf16[1024,300]{0,1:T(8,128)(2,1)}, u32[]{:S(2)}) copy-start(bf16[1024,300]{0,1:T(8,128)(2,1)} %param.10) | copy-start | bytes 1843204
  98.8 6.8 %copy-start.5 = (f32[1024,300]{0,1:T(8,128)S(1)}, f32[1024,300]{0,1:T(8,128)}, u32[]{:S(2)}) copy-start(f32[1024,300]{0,1:T(8,128)} %param.12) | copy-start | bytes 3686404
  103.8 1.7 %collective-permute-start.16 = (bf16[160,1024]{1,0:T(8,128)(2,1)S(1)}, bf16[160,1024]{1,0:T(8,128)(2,1)S(1)}, u32[]{:S(2)}, u32[]{:S(2)}) collective-permute-start(bf16[160,1024]{1,0:T(8,128)(2,1)S(1)} %add_convert_fusion), channel_id=1, source_target_pairs={{0,1},{1,0},{2,3},{3,2},{4,5},{5,4},{6,7},{7,6},{8,9},{9,8},{10,11... | collective-permute-start | bytes 983048 | tf_op jit(solution)/shard_map/col_other/ppermute | solution.py:36
where the time goes:
time: 107 us
  waiting for transfers between devices  35.8 us (33%)
  starting transfers between devices  34.6 us (32%)
  Pallas kernels  26.5 us (25%)
  other arithmetic  4.71 us (4%)
  local copies, waits for them, and re-layouts  4.26 us (4%)
    ppermute x17, waiting for transfers between devices, hop(): return lax.ppermute(array, AXES, perm)  35.8 us
    ppermute x17, starting transfers between devices, hop(): return lax.ppermute(array, AXES, perm)  34.6 us
    pallas_call x1, Pallas kernels, first_pair(): pl.pallas_call(first_kernel, out_shape=(shape(LOW), shape(LOW), shape(WID...  9.91 us
    pallas_call x1, Pallas kernels, second_pair(): pl.pallas_call(second_kernel, out_shape=(vmem(LOW), vmem(LOW), shape(LOW)...  8.04 us
    unnamed x14, local copies, waits for them, and re-layouts  4.26 us
    pallas_call x1, Pallas kernels, pick_rows(): pl.pallas_call(rows_kernel, out_shape=(shape(WIDE), shape(WIDE)), in_spec...  3.43 us
    pallas_call x1, Pallas kernels, weigh(): pl.pallas_call(weigh_kernel, out_shape=jax.ShapeDtypeStruct((2, TERMS, TE...  3.19 us
  transfers between devices with their start and end apart: 17, of which 7 were waited for; matrix products, arithmetic and copies ran while one was open for 3% of the time, Pallas kernels for 15%

commit v1 on v0

v1 whole, which is shorter than its diff:
```python
import jax
import jax.numpy as jnp
from jax import lax
from jax.experimental import pallas as pl
from jax.experimental.pallas import tpu as pltpu
from jax.sharding import PartitionSpec as P

LEARN_RATE = 0.05
DIM = 300
WIDE = 304
LOW = 160
HIGH = WIDE - LOW
FULL = DIM // 16 * 16
OFF = DIM
ONE = DIM + 1
DIGIT = 32
TERMS = 1024
RING = 8
STRIDE = 8
AXES = ("blk", "rep")
F32 = jnp.float32
BF16 = jnp.bfloat16


def hop(name, array, moves):
    perm = []
    for blk in range(RING * STRIDE):
        for rep in range(4):
            if moves[rep] is None:
                continue
            by, to = moves[rep]
            dst = (blk + STRIDE * by) % (RING * STRIDE)
            perm.append((blk * 4 + rep, dst * 4 + to))
    with jax.named_scope(name):
        return lax.ppermute(array, AXES, perm)


CORE = [(0, 1), (0, 0), (0, 3), (0, 2)]
ACROSS = [(0, 2), (0, 3), (0, 0), (0, 1)]


def dot(a, b, ca, cb):
    return lax.dot_general(a, b, (((ca,), (cb,)), ((), ())), preferred_element_type=F32)


def one_hot(index):
    hit = lax.broadcasted_iota(jnp.int32, (TERMS, TERMS), 0) == index
    return jnp.where(hit, 1.0, 0.0).astype(BF16)


def shape(rows, dtype=BF16):
    return jax.ShapeDtypeStruct((rows, TERMS), dtype)


def vmem(rows, dtype=BF16):
    return pltpu.VMEM((rows, TERMS), dtype)


def cost(flops, moved, trans=0):
    return pl.CostEstimate(flops=flops, bytes_accessed=moved, transcendentals=trans)


MATMUL = 2 * WIDE * TERMS * TERMS


def last_rows(emb_ref, tail, rows):
    left = DIM - FULL
    tail[:left] = emb_ref[FULL:DIM].astype(F32)
    for i, row in enumerate(rows):
        tail[left + i : left + i + 1] = row
    return tail[...].astype(BF16)


def order(ref, swap):
    idx = ref[...].reshape(2, TERMS)
    one, two = idx[:1], idx[1:]
    return jnp.where(swap, two, one), jnp.where(swap, one, two)


def pack_kernel(swap_ref, emb_ref, off_ref, idx_ref, out_ref, idx_out, tail):
    idx, idx_2 = order(idx_ref, swap_ref[0] == 1)
    idx_out[...] = idx_2
    zero = jnp.zeros((1, TERMS), F32)
    high = (idx // DIGIT).astype(F32)
    low = (idx % DIGIT).astype(F32)
    off = off_ref[...].astype(F32).reshape(1, TERMS)
    out_ref[:FULL] = emb_ref[:FULL]
    out_ref[FULL:] = last_rows(emb_ref, tail, [off, high, low, zero])


KERNEL_VMEM = 32 * 2**20
VMEM = pl.BlockSpec(memory_space=pltpu.VMEM)
SMEM = pl.BlockSpec(memory_space=pltpu.SMEM)
HBM = pl.BlockSpec(memory_space=pltpu.HBM)


def pack(swap, emb, off, idx):
    return pl.pallas_call(
        pack_kernel,
        out_shape=(shape(WIDE), shape(1, jnp.int32)),
        in_specs=[SMEM] + [VMEM] * 3,
        out_specs=(VMEM,) * 2,
        scratch_shapes=[pltpu.VMEM((16, TERMS), F32)],
        cost_estimate=cost(0, 1300000),
    )(swap, emb, off, idx)


def rows_kernel(swap_ref, emb_ref, off_ref, idx_ref, row_1, row_2, wide, tail):
    zero = jnp.zeros((1, TERMS), F32)
    off = off_ref[...].astype(F32).reshape(1, TERMS)
    wide[:FULL] = emb_ref[:FULL]
    wide[FULL:] = last_rows(emb_ref, tail, [zero + 1.0, off, zero, zero])
    for idx, out in zip(order(idx_ref, swap_ref[0] == 1), (row_1, row_2)):
        out[...] = dot(wide[...], one_hot(idx), 1, 0).astype(BF16)


def pick_rows(swap, emb, off, idx):
    return pl.pallas_call(
        rows_kernel,
        out_shape=(shape(WIDE), shape(WIDE)),
        in_specs=[SMEM] + [VMEM] * 3,
        out_specs=(VMEM,) * 2,
        scratch_shapes=[pltpu.VMEM((WIDE, TERMS), BF16), pltpu.VMEM((16, TERMS), F32)],
        cost_estimate=cost(2 * MATMUL, 2000000),
    )(swap, emb, off, idx)


def weights(count):
    scale = 1.0 / TERMS
    count_f = count.astype(F32)
    slope = 0.1 * scale + (0.25 * scale) * (count_f * lax.rsqrt(count_f))
    base = slope * jnp.log(count_f)
    return jnp.where(count > 0, slope, 0.0), jnp.where(count > 0, base, 0.0)


def cells(score, slope, base):
    scale = 0.5 / TERMS
    unseen = scale + scale * jnp.tanh(0.5 * score)
    return jnp.where(slope > 0, slope * score - base, unseen).astype(BF16)


def start(src, dst, sem):
    copy = pltpu.make_async_copy(src, dst, sem)
    copy.start()
    return copy


def score(pair, idx, block, counts_ref, row_ref, row_idx, counts, row, cell_buf, sems):
    get_row = start(row_ref, row, sems.at[0])
    get_counts = start(counts_ref.at[pair], counts, sems.at[1])
    pick = one_hot(idx)
    col = dot(block, pick, 1, 0)
    at = lax.broadcasted_iota(jnp.int32, (WIDE, TERMS), 0)
    col = jnp.where(at > OFF, jnp.where(at == ONE, 1.0, 0.0), col).astype(BF16)
    get_row.wait()
    est = dot(row[...], col, 0, 0)
    get_counts.wait()
    cell_buf[...] = cells(est, *weights(counts[...]))
    grad = dot(row[...], cell_buf[...], 1, 0).astype(BF16)
    grad = dot(grad, pick, 1, 1).astype(BF16)
    row_part = dot(col, cell_buf[...], 1, 1).astype(BF16)
    return grad, dot(row_part, one_hot(row_idx), 1, 1)


SCORE_SCRATCH = [
    pltpu.VMEM((TERMS, TERMS), jnp.int32),
    pltpu.VMEM((WIDE, TERMS), BF16),
    pltpu.VMEM((TERMS, TERMS), BF16),
    pltpu.SemaphoreType.DMA((3,)),
    pltpu.VMEM((WIDE, TERMS), F32),
]


def first_kernel(
    swap_ref, counts_ref, row_ref, row_idx_ref, block_ref, col_out, row_out,
    counts, row, cell_buf, sems, total,
):
    swap = swap_ref[0]
    digits = block_ref[FULL:].astype(F32)
    one = ONE - FULL
    idx = (digits[one : one + 1] * DIGIT + digits[one + 1 : one + 2]).astype(jnp.int32)
    row_idx = order(row_idx_ref, swap == 1)[0]
    grad, total[...] = score(
        swap, idx, block_ref[...], counts_ref, row_ref, row_idx, counts, row, cell_buf, sems
    )
    put = start(total, row_out, sems.at[2])
    col_out[...] = grad
    put.wait()


def first_pair(swap, *args):
    return pl.pallas_call(
        first_kernel,
        out_shape=(vmem(WIDE), pltpu.HBM((WIDE, TERMS), F32)),
        in_specs=[SMEM, HBM, HBM, VMEM, VMEM],
        out_specs=(VMEM, HBM),
        scratch_shapes=SCORE_SCRATCH,
        compiler_params=pltpu.CompilerParams(vmem_limit_bytes=KERNEL_VMEM),
        cost_estimate=cost(6 * MATMUL, 12000000, 3 * TERMS * TERMS),
    )(swap, *args)


def put_halves(value, low_out, high_out):
    low_out[...] = value[:LOW]
    high_out[:HIGH] = value[LOW:]
    high_out[HIGH:] = jnp.zeros((LOW - HIGH, TERMS), BF16)


def second_kernel(
    swap_ref, counts_ref, row_ref, prev_ref, row_idx_ref, idx_ref, block_ref, block_2_ref,
    low_out, high_out, row_low_out, row_high_out, counts, row, cell_buf, sems, prev,
):
    swap = swap_ref[0]
    get_prev = start(prev_ref, prev, sems.at[2])
    row_idx = order(row_idx_ref, swap == 1)[1]
    block = block_ref[...] + block_2_ref[...]
    grad, total = score(
        1 - swap, idx_ref[...], block, counts_ref, row_ref, row_idx, counts, row, cell_buf, sems
    )
    low_out[...] = grad[:LOW]
    high_out[...] = grad[LOW:]
    get_prev.wait()
    put_halves((prev[...] + total).astype(BF16), row_low_out, row_high_out)


def second_pair(swap, *args):
    return pl.pallas_call(
        second_kernel,
        out_shape=(vmem(LOW), vmem(HIGH), shape(LOW), shape(LOW)),
        in_specs=[SMEM] + [HBM] * 3 + [VMEM] * 4,
        out_specs=(VMEM,) * 4,
        scratch_shapes=SCORE_SCRATCH,
        compiler_params=pltpu.CompilerParams(vmem_limit_bytes=KERNEL_VMEM),
        cost_estimate=cost(6 * MATMUL, 12000000, 3 * TERMS * TERMS),
    )(swap, *args)


def adagrad(core, mine, other, table, acc):
    low = jnp.where(core == 0, mine, other)
    high = jnp.where(core == 0, other, mine)[: DIM - LOW]
    total = jnp.concatenate([low, high]).astype(F32)
    step = LEARN_RATE * total * lax.rsqrt(acc + total * total)
    return (table.astype(F32) - step).astype(BF16)


def in_hbm(array):
    return pltpu.with_memory_space_constraint(array, pltpu.HBM)


def halves(core, low, high):
    return jnp.where(core == 0, low, high), jnp.where(core == 0, high, low)


def add(*parts):
    total = parts[0].astype(F32)
    for part in parts[1:]:
        total = total + part.astype(F32)
    return total.astype(BF16)


def per_device(
    row_emb, col_emb, row_acc, col_acc, row_offset, col_offset, counts, row_index, col_index
):
    replica = lax.axis_index("rep")
    core = replica & 1
    is_0, is_3 = replica == 0, replica == 3
    swap = is_3.astype(jnp.int32).reshape(1)
    counts = in_hbm(counts.reshape(counts.shape[2:]))

    barrier = lax.optimization_barrier
    block, col_idx_2 = pack(swap, col_emb.T, col_offset, col_index)
    got = hop("got", block, [(0, 0), (-1, 1), (-2, 2), (1, 3)])
    far = hop("far", block, [None, (3, 1), None, None])
    idx_2 = hop("idx_2", col_idx_2, [(-4, 0), (3, 1), (2, 2), (-3, 3)])
    row_1, row_2 = pick_rows(swap, row_emb.T, row_offset, row_index)
    got, row_1 = barrier((got, row_1))
    near = hop("near", got, [None, (-3, 0), (-1, 3), (1, 2)])
    grad_1, row_sum = first_pair(swap, counts, in_hbm(row_1), row_index, got)
    near, far, idx_2, grad_1 = barrier((near, far, idx_2, grad_1))
    low, high, row_low, row_high = second_pair(
        swap, counts, in_hbm(row_2), in_hbm(row_sum), row_index, idx_2, far, near
    )

    way = [(3, 1), (-3, 0), (-1, 3), (1, 2)]
    low = hop("low", low, way)
    high = hop("high", high, way)
    row_keep, row_give = halves(core, row_low, row_high)
    row_chip = add(row_keep, hop("row_swap", row_give, CORE))
    low, row_chip = barrier((low, row_chip))
    low = add(grad_1[:LOW], low)
    low_up = hop("low_up", low, [None, (1, 0), (2, 2), None])
    low_down = hop("low_down", low, [None, None, None, (-1, 2)])
    high = add(grad_1[LOW:], high)
    high_up = hop("high_up", high, [None, (1, 1), (2, 3), None])
    high_down = hop("high_down", high, [(0, 1), None, None, (-1, 3)])
    low = add(low_up, low_down, jnp.where(is_0, low, 0))
    high = jnp.pad(add(high_up, high_down), ((0, LOW - HIGH), (0, 0)))
    col_chip = halves(core, low, high)[0]
    col_across = hop("col_across", col_chip, ACROSS)
    row_across = hop("row_across", row_chip, ACROSS)
    col_across, row_across = barrier((col_across, row_across))
    row_mine = add(row_chip, row_across)
    row_other = hop("row_other", row_mine, CORE)
    new_row = adagrad(core, row_mine, row_other, row_emb.T, row_acc.T)
    col_mine = add(col_chip, col_across)
    col_other = hop("col_other", col_mine, CORE)
    new_col = adagrad(core, col_mine, col_other, col_emb.T, col_acc.T)
    return (new_row.T, new_col.T)


def solution(mesh):
    in_specs = (
        P("blk", None),
        P("blk", None),
        P("blk", None),
        P("blk", None),
        P("blk"),
        P("blk"),
        P("blk", "rep", None, None, None),
        P("blk", "rep", None, None),
        P("blk", "rep", None, None),
    )
    out_specs = (P("blk", None), P("blk", None))
    return jax.shard_map(
        per_device, mesh=mesh, in_specs=in_specs, out_specs=out_specs, check_vma=False
    )
```

time: 107 us -> 102 us (0.953)
  waiting for transfers between devices: 35.8 us -> 40.5 us
  Pallas kernels: 26.5 us -> 22.7 us
  local copies, waits for them, and re-layouts: 4.26 us -> 1.39 us
  starting transfers between devices: 34.6 us -> 32 us
  other arithmetic: 4.71 us -> 3.41 us
    ppermute x17 -> x15, waiting for transfers between devices: 35.8 us -> 40.5 us  [hop(): return lax.ppermute(array, AXES, perm)]
    pallas_call x4 -> x3, Pallas kernels: 23.1 us -> 19.3 us  [the longest x1 8.72 us: second_pair(): pl.pallas_call(second_kernel, out_shape=(vmem(LOW), vmem(HIGH), shape(LOW...]
    unnamed x14 -> x12, local copies, waits for them, and re-layouts: 4.26 us -> 1.39 us
    ppermute x17 -> x15, starting transfers between devices: 34.6 us -> 32 us  [hop(): return lax.ppermute(array, AXES, perm)]
    convert_element_type x6, other arithmetic: 1.82 us -> 0.61 us  [add(): return total.astype(BF16)]
    convert_element_type x1 -> x0, other arithmetic: 1.21 us -> none  [adagrad(): return (table.astype(F32) - step).astype(BF16)]
    transpose x1 -> x2, other arithmetic: 1.2 us -> 2.4 us  [per_device(): return (new_row.T, new_col.T)]
  transfers between devices with their start and end apart: 17 -> 15, of which waited for: 7 -> 9; matrix products, arithmetic and copies ran while one was open for 3% -> 2% of each run, Pallas kernels for 15% -> 12%
where the time goes in v1:
time: 102 us; the launch traced here: 101 us
  waiting for transfers between devices  40.5 us (40%)
  starting transfers between devices  32 us (31%)
  Pallas kernels  22.7 us (22%)
  other arithmetic  3.41 us (3%)
  local copies, waits for them, and re-layouts  1.39 us (1%)
    ppermute x15, waiting for transfers between devices, hop(): return lax.ppermute(array, AXES, perm)  40.5 us
    ppermute x15, starting transfers between devices, hop(): return lax.ppermute(array, AXES, perm)  32 us
    pallas_call x1, Pallas kernels, second_pair(): pl.pallas_call(second_kernel, out_shape=(vmem(LOW), vmem(HIGH), shape(LOW...  8.72 us
    pallas_call x1, Pallas kernels, first_pair(): pl.pallas_call(first_kernel, out_shape=(vmem(WIDE), pltpu.HBM((WIDE, TERM...  8.54 us
    pallas_call x1, Pallas kernels, pick_rows(): pl.pallas_call(rows_kernel, out_shape=(shape(WIDE), shape(WIDE)), in_spec...  3.44 us
    transpose x2, other arithmetic, per_device(): return (new_row.T, new_col.T)  2.4 us
  transfers between devices with their start and end apart: 15, of which 9 were waited for; matrix products, arithmetic and copies ran while one was open for 2% of the time, Pallas kernels for 12%

profile of v1, /device:TPU:1, one launch (start us, length us, event | category | flops | bytes accessed | tf_op | source)
XLA Modules:
  0.0 100.9 jit_solution(14950976098948481184)
XLA Ops:
  0.6 2.0 %shard_map.105 = (bf16[304,1024]{1,0:T(8,128)(2,1)}, s32[1,1024]{1,0:T(1,128)}) custom-call(s32[1]{0:T(128)} %bitcast.1.swap_ref, bf16[300,1024]{1,0:T(8,128)(2,1)} %bitcast.18, bf16[1024]{0:T(1024)(128)(2,1)} %off_ref.3, s32[1,1,2,1024]{3,2,1,0:T(2,128)} %idx_ref.3), custom_call_target="tpu_custom_call" | custom-call | bytes 1300000 | tf_op jit(solution)/shard_map/pallas_call | solution.py:98
  2.6 8.3 %collective-permute-start = (bf16[304,1024]{1,0:T(8,128)(2,1)}, bf16[304,1024]{1,0:T(8,128)(2,1)S(1)}, u32[]{:S(2)}, u32[]{:S(2)}) collective-permute-start(bf16[304,1024]{1,0:T(8,128)(2,1)} %get-tuple-element.23), channel_id=1, source_target_pairs={{0,0},{1,225},{2,194},{3,35},{4,4},{5,229},{6,198},{7,39},{8,8},{9... | collective-permute-start | bytes 1867784 | tf_op jit(solution)/shard_map/got/ppermute | solution.py:35
  10.9 1.9 %collective-permute-start.2 = (bf16[304,1024]{1,0:T(8,128)(2,1)}, bf16[304,1024]{1,0:T(8,128)(2,1)S(1)}, u32[]{:S(2)}, u32[]{:S(2)}) collective-permute-start(bf16[304,1024]{1,0:T(8,128)(2,1)} %get-tuple-element.23), channel_id=1, source_target_pairs={{1,97},{5,101},{9,105},{13,109},{17,113},{21,117},{25,121},{29,125... | collective-permute-start | bytes 1867784 | tf_op jit(solution)/shard_map/far/ppermute | solution.py:35
  12.9 3.4 %shard_map.104 = (bf16[304,1024]{1,0:T(8,128)(2,1)}, bf16[304,1024]{1,0:T(8,128)(2,1)}) custom-call(s32[1]{0:T(128)} %bitcast.1.swap_ref, bf16[300,1024]{1,0:T(8,128)(2,1)} %bitcast.19, bf16[1024]{0:T(1024)(128)(2,1)} %off_ref.2, s32[1,1,2,1024]{3,2,1,0:T(2,128)} %row_idx_ref.3), custom_call_target="tpu_custom_call" | custom-call | flops 1275068416 | bytes 2000000 | tf_op jit(solution)/shard_map/pallas_call | solution.py:118
  16.3 2.1 %collective-permute-done.block_ref = bf16[304,1024]{1,0:T(8,128)(2,1)S(1)} collective-permute-done((bf16[304,1024]{1,0:T(8,128)(2,1)}, bf16[304,1024]{1,0:T(8,128)(2,1)S(1)}, u32[]{:S(2)}, u32[]{:S(2)}) %collective-permute-start) | collective-permute-done | bytes 622624 | tf_op jit(solution)/shard_map/got/ppermute | solution.py:35
  18.4 1.3 %collective-permute-start.1 = (bf16[304,1024]{1,0:T(8,128)(2,1)S(1)}, bf16[304,1024]{1,0:T(8,128)(2,1)S(1)}, u32[]{:S(2)}, u32[]{:S(2)}) collective-permute-start(bf16[304,1024]{1,0:T(8,128)(2,1)S(1)} %collective-permute-done.block_ref), channel_id=1, source_target_pairs={{1,160},{2,227},{3,34},{5,164},{6,231},{7,38},{9,168},{10,235},{11... | collective-permute-start | bytes 1867784 | tf_op jit(solution)/shard_map/near/ppermute | solution.py:35
  19.7 2.2 %collective-permute-start.3 = (s32[1,1024]{1,0:T(1,128)S(1)}, s32[1,1024]{1,0:T(1,128)S(1)}, u32[]{:S(2)}, u32[]{:S(2)}) collective-permute-start(s32[1,1024]{1,0:T(1,128)S(1)} %copy-done.5), channel_id=1, source_target_pairs={{0,128},{1,97},{2,66},{3,163},{4,132},{5,101},{6,70},{7,167},{8,13... | collective-permute-start | bytes 12296 | tf_op jit(solution)/shard_map/idx_2/ppermute | solution.py:35
  22.0 8.5 %shard_map.106 = (bf16[304,1024]{1,0:T(8,128)(2,1)S(1)}, f32[304,1024]{1,0:T(8,128)}) custom-call(s32[1]{0:T(128)} %bitcast.1.swap_ref, s32[2,1024,1024]{2,1,0:T(8,128)} %bitcast.20, bf16[304,1024]{1,0:T(8,128)(2,1)} %get-tuple-element.25.row_ref, s32[1,1,2,1024]{3,2,1,0:T(2,128)S(1)} %copy-done, bf16[304,1024]{1,0:T(8,128)(2,1)S(1)} %collective-permute-done.block_ref), custom_call_target="tpu_custom_call" | custom-call | flops 3825205248 | bytes 12000000 | tf_op jit(solution)/shard_map/pallas_call | solution.py:192
  30.5 6.2 %collective-permute-done.3.idx_ref = s32[1,1024]{1,0:T(1,128)S(1)} collective-permute-done((s32[1,1024]{1,0:T(1,128)S(1)}, s32[1,1024]{1,0:T(1,128)S(1)}, u32[]{:S(2)}, u32[]{:S(2)}) %collective-permute-start.3) | collective-permute-done | bytes 4128 | tf_op jit(solution)/shard_map/idx_2/ppermute | solution.py:35
  36.7 2.6 %collective-permute-done.1.block_2_ref = bf16[304,1024]{1,0:T(8,128)(2,1)S(1)} collective-permute-done((bf16[304,1024]{1,0:T(8,128)(2,1)S(1)}, bf16[304,1024]{1,0:T(8,128)(2,1)S(1)}, u32[]{:S(2)}, u32[]{:S(2)}) %collective-permute-start.1) | collective-permute-done | bytes 622624 | tf_op jit(solution)/shard_map/near/ppermute | solution.py:35
  39.3 8.7 %shard_map.107 = (bf16[160,1024]{1,0:T(8,128)(2,1)S(1)}, bf16[144,1024]{1,0:T(8,128)(2,1)S(1)}, bf16[160,1024]{1,0:T(8,128)(2,1)S(1)}, bf16[160,1024]{1,0:T(8,128)(2,1)S(1)}) custom-call(s32[1]{0:T(128)} %bitcast.1.swap_ref, s32[2,1024,1024]{2,1,0:T(8,128)} %bitcast.21, bf16[304,1024]{1,0:T(8,128)(2,1)} %get-tuple-element.22.row_ref, ...), custom_call_target="tpu_custom_call" | custom-call | flops 3825205248 | bytes 12000000 | tf_op jit(solution)/shard_map/pallas_call | solution.py:227
  48.1 5.6 %collective-permute-start.8 = (bf16[144,1024]{1,0:T(8,128)(2,1)S(1)}, bf16[144,1024]{1,0:T(8,128)(2,1)S(1)}, u32[]{:S(2)}, u32[]{:S(2)}) collective-permute-start(bf16[144,1024]{1,0:T(8,128)(2,1)S(1)} %get-tuple-element.39), channel_id=1, source_target_pairs={{0,97},{1,160},{2,227},{3,34},{4,101},{5,164},{6,231},{7,38},{8,10... | collective-permute-start | bytes 884744 | tf_op jit(solution)/shard_map/high/ppermute | solution.py:35
  53.8 3.8 %collective-permute-start.4 = (bf16[160,1024]{1,0:T(8,128)(2,1)S(1)}, bf16[160,1024]{1,0:T(8,128)(2,1)S(1)}, u32[]{:S(2)}, u32[]{:S(2)}) collective-permute-start(bf16[160,1024]{1,0:T(8,128)(2,1)S(1)} %get-tuple-element.33), channel_id=1, source_target_pairs={{0,97},{1,160},{2,227},{3,34},{4,101},{5,164},{6,231},{7,38},{8,10... | collective-permute-start | bytes 983048 | tf_op jit(solution)/shard_map/low/ppermute | solution.py:35
  57.6 8.1 %collective-permute-done.8 = bf16[144,1024]{1,0:T(8,128)(2,1)S(1)} collective-permute-done((bf16[144,1024]{1,0:T(8,128)(2,1)S(1)}, bf16[144,1024]{1,0:T(8,128)(2,1)S(1)}, u32[]{:S(2)}, u32[]{:S(2)}) %collective-permute-start.8) | collective-permute-done | bytes 294944 | tf_op jit(solution)/shard_map/high/ppermute | solution.py:35
  65.7 1.3 %collective-permute-start.10 = (bf16[144,1024]{1,0:T(8,128)(2,1)S(1)}, bf16[144,1024]{1,0:T(8,128)(2,1)S(1)}, u32[]{:S(2)}, u32[]{:S(2)}) collective-permute-start(bf16[144,1024]{1,0:T(8,128)(2,1)S(1)} %add_convert_fusion.6), channel_id=1, source_target_pairs={{0,1},{3,227},{4,5},{7,231},{8,9},{11,235},{12,13},{15,239},{16,17... | collective-permute-start | bytes 884744 | tf_op jit(solution)/shard_map/high_down/ppermute | solution.py:35
  67.0 2.4 %collective-permute-start.9 = (bf16[144,1024]{1,0:T(8,128)(2,1)S(1)}, bf16[144,1024]{1,0:T(8,128)(2,1)S(1)}, u32[]{:S(2)}, u32[]{:S(2)}) collective-permute-start(bf16[144,1024]{1,0:T(8,128)(2,1)S(1)} %add_convert_fusion.6), channel_id=1, source_target_pairs={{1,33},{2,67},{5,37},{6,71},{9,41},{10,75},{13,45},{14,79},{17,49}... | collective-permute-start | bytes 884744 | tf_op jit(solution)/shard_map/high_up/ppermute | solution.py:35
  69.6 6.6 %collective-permute-done.4 = bf16[160,1024]{1,0:T(8,128)(2,1)S(1)} collective-permute-done((bf16[160,1024]{1,0:T(8,128)(2,1)S(1)}, bf16[160,1024]{1,0:T(8,128)(2,1)S(1)}, u32[]{:S(2)}, u32[]{:S(2)}) %collective-permute-start.4) | collective-permute-done | bytes 327712 | tf_op jit(solution)/shard_map/low/ppermute | solution.py:35
  76.3 3.6 %collective-permute-start.6 = (bf16[160,1024]{1,0:T(8,128)(2,1)S(1)}, bf16[160,1024]{1,0:T(8,128)(2,1)S(1)}, u32[]{:S(2)}, u32[]{:S(2)}) collective-permute-start(bf16[160,1024]{1,0:T(8,128)(2,1)S(1)} %add_convert_fusion.3), channel_id=1, source_target_pairs={{1,32},{2,66},{5,36},{6,70},{9,40},{10,74},{13,44},{14,78},{17,48}... | collective-permute-start | bytes 983048 | tf_op jit(solution)/shard_map/low_up/ppermute | solution.py:35
  80.8 3.1 %collective-permute-done.6 = bf16[160,1024]{1,0:T(8,128)(2,1)S(1)} collective-permute-done((bf16[160,1024]{1,0:T(8,128)(2,1)S(1)}, bf16[160,1024]{1,0:T(8,128)(2,1)S(1)}, u32[]{:S(2)}, u32[]{:S(2)}) %collective-permute-start.6) | collective-permute-done | bytes 327712 | tf_op jit(solution)/shard_map/low_up/ppermute | solution.py:35
  84.2 4.6 %collective-permute-done.12 = bf16[160,1024]{1,0:T(8,128)(2,1)S(1)} collective-permute-done((bf16[160,1024]{1,0:T(8,128)(2,1)S(1)}, bf16[160,1024]{1,0:T(8,128)(2,1)S(1)}, u32[]{:S(2)}, u32[]{:S(2)}) %collective-permute-start.12) | collective-permute-done | bytes 327712 | tf_op jit(solution)/shard_map/row_across/ppermute | solution.py:35
  88.8 6.3 %collective-permute-done.11 = bf16[160,1024]{1,0:T(8,128)(2,1)S(1)} collective-permute-done((bf16[160,1024]{1,0:T(8,128)(2,1)S(1)}, bf16[160,1024]{1,0:T(8,128)(2,1)S(1)}, u32[]{:S(2)}, u32[]{:S(2)}) %collective-permute-start.11) | collective-permute-done | bytes 327712 | tf_op jit(solution)/shard_map/col_across/ppermute | solution.py:35
  97.1 1.2 %fusion.10 = bf16[1024,300]{0,1:T(8,128)(2,1)} fusion(f32[1024,300]{0,1:T(8,128)S(1)} %copy-done.2, bf16[140,1024]{1,0:T(8,128)(2,1)S(1)} %slice_select_fusion, bf16[160,1024]{1,0:T(8,128)(2,1)S(1)} %broadcast_select_fusion, bf16[1024,300]{0,1:T(8,128)(2,1)S(1)} %copy-done.1), kind=kLoop, calls=%fused_computation.19 | loop fusion | flops 3379200 | bytes 3072000 | tf_op jit(solution)/shard_map/transpose | solution.py:308
  98.3 1.2 %copy-done.3 = f32[1024,300]{0,1:T(8,128)S(1)} copy-done((f32[1024,300]{0,1:T(8,128)S(1)}, f32[1024,300]{0,1:T(8,128)}, u32[]{:S(2)}) %copy-start.3) | copy-done | bytes 1228824
  99.7 1.2 %fusion.11 = bf16[1024,300]{0,1:T(8,128)(2,1)} fusion(f32[1024,300]{0,1:T(8,128)S(1)} %copy-done.3, bf16[140,1024]{1,0:T(8,128)(2,1)S(1)} %slice_select_fusion.1, bf16[160,1024]{1,0:T(8,128)(2,1)S(1)} %broadcast_select_fusion.1, bf16[1024,300]{0,1:T(8,128)(2,1)S(1)} %copy-done.4), kind=kLoop, calls=%fused_computation.20 | loop fusion | flops 3379200 | bytes 3072000 | tf_op jit(solution)/shard_map/transpose | solution.py:308
  (36 shorter events, 3.8 us)
Async XLA Ops:
  2.6 15.8 %collective-permute-start = (bf16[304,1024]{1,0:T(8,128)(2,1)}, bf16[304,1024]{1,0:T(8,128)(2,1)S(1)}, u32[]{:S(2)}, u32[]{:S(2)}) collective-permute-start(bf16[304,1024]{1,0:T(8,128)(2,1)} %get-tuple-element.23), channel_id=1, source_target_pairs={{0,0},{1,225},{2,194},{3,35},{4,4},{5,229},{6,198},{7,39},{8,8},{9... | collective-permute-start | bytes 1867784 | tf_op jit(solution)/shard_map/got/ppermute | solution.py:35
  10.9 25.8 %collective-permute-start.2 = (bf16[304,1024]{1,0:T(8,128)(2,1)}, bf16[304,1024]{1,0:T(8,128)(2,1)S(1)}, u32[]{:S(2)}, u32[]{:S(2)}) collective-permute-start(bf16[304,1024]{1,0:T(8,128)(2,1)} %get-tuple-element.23), channel_id=1, source_target_pairs={{1,97},{5,101},{9,105},{13,109},{17,113},{21,117},{25,121},{29,125... | collective-permute-start | bytes 1867784 | tf_op jit(solution)/shard_map/far/ppermute | solution.py:35
  12.9 6.9 %copy-start.5 = (s32[1,1024]{1,0:T(1,128)S(1)}, s32[1,1024]{1,0:T(1,128)}, u32[]{:S(2)}) copy-start(s32[1,1024]{1,0:T(1,128)} %get-tuple-element.28) | copy-start | bytes 12292
  12.9 9.1 %copy-start = (s32[1,1,2,1024]{3,2,1,0:T(2,128)S(1)}, s32[1,1,2,1024]{3,2,1,0:T(2,128)}, u32[]{:S(2)}) copy-start(s32[1,1,2,1024]{3,2,1,0:T(2,128)} %row_idx_ref.3) | copy-start | bytes 24580
  18.4 20.9 %collective-permute-start.1 = (bf16[304,1024]{1,0:T(8,128)(2,1)S(1)}, bf16[304,1024]{1,0:T(8,128)(2,1)S(1)}, u32[]{:S(2)}, u32[]{:S(2)}) collective-permute-start(bf16[304,1024]{1,0:T(8,128)(2,1)S(1)} %collective-permute-done.block_ref), channel_id=1, source_target_pairs={{1,160},{2,227},{3,34},{5,164},{6,231},{7,38},{9,168},{10,235},{11... | collective-permute-start | bytes 1867784 | tf_op jit(solution)/shard_map/near/ppermute | solution.py:35
  19.7 17.0 %collective-permute-start.3 = (s32[1,1024]{1,0:T(1,128)S(1)}, s32[1,1024]{1,0:T(1,128)S(1)}, u32[]{:S(2)}, u32[]{:S(2)}) collective-permute-start(s32[1,1024]{1,0:T(1,128)S(1)} %copy-done.5), channel_id=1, source_target_pairs={{0,128},{1,97},{2,66},{3,163},{4,132},{5,101},{6,70},{7,167},{8,13... | collective-permute-start | bytes 12296 | tf_op jit(solution)/shard_map/idx_2/ppermute | solution.py:35
  48.1 17.6 %collective-permute-start.8 = (bf16[144,1024]{1,0:T(8,128)(2,1)S(1)}, bf16[144,1024]{1,0:T(8,128)(2,1)S(1)}, u32[]{:S(2)}, u32[]{:S(2)}) collective-permute-start(bf16[144,1024]{1,0:T(8,128)(2,1)S(1)} %get-tuple-element.39), channel_id=1, source_target_pairs={{0,97},{1,160},{2,227},{3,34},{4,101},{5,164},{6,231},{7,38},{8,10... | collective-permute-start | bytes 884744 | tf_op jit(solution)/shard_map/high/ppermute | solution.py:35
  53.7 15.8 %collective-permute-start.5 = (bf16[160,1024]{1,0:T(8,128)(2,1)S(1)}, bf16[160,1024]{1,0:T(8,128)(2,1)S(1)}, u32[]{:S(2)}, u32[]{:S(2)}) collective-permute-start(bf16[160,1024]{1,0:T(8,128)(2,1)S(1)} %broadcast_select_fusion.2), channel_id=1, source_target_pairs={{0,1},{1,0},{2,3},{3,2},{4,5},{5,4},{6,7},{7,6},{8,9},{9,8},{10,11... | collective-permute-start | bytes 983048 | tf_op jit(solution)/shard_map/row_swap/ppermute | solution.py:35
  53.8 22.4 %collective-permute-start.4 = (bf16[160,1024]{1,0:T(8,128)(2,1)S(1)}, bf16[160,1024]{1,0:T(8,128)(2,1)S(1)}, u32[]{:S(2)}, u32[]{:S(2)}) collective-permute-start(bf16[160,1024]{1,0:T(8,128)(2,1)S(1)} %get-tuple-element.33), channel_id=1, source_target_pairs={{0,97},{1,160},{2,227},{3,34},{4,101},{5,164},{6,231},{7,38},{8,10... | collective-permute-start | bytes 983048 | tf_op jit(solution)/shard_map/low/ppermute | solution.py:35
  65.7 15.0 %collective-permute-start.10 = (bf16[144,1024]{1,0:T(8,128)(2,1)S(1)}, bf16[144,1024]{1,0:T(8,128)(2,1)S(1)}, u32[]{:S(2)}, u32[]{:S(2)}) collective-permute-start(bf16[144,1024]{1,0:T(8,128)(2,1)S(1)} %add_convert_fusion.6), channel_id=1, source_target_pairs={{0,1},{3,227},{4,5},{7,231},{8,9},{11,235},{12,13},{15,239},{16,17... | collective-permute-start | bytes 884744 | tf_op jit(solution)/shard_map/high_down/ppermute | solution.py:35
  67.0 13.7 %collective-permute-start.9 = (bf16[144,1024]{1,0:T(8,128)(2,1)S(1)}, bf16[144,1024]{1,0:T(8,128)(2,1)S(1)}, u32[]{:S(2)}, u32[]{:S(2)}) collective-permute-start(bf16[144,1024]{1,0:T(8,128)(2,1)S(1)} %add_convert_fusion.6), channel_id=1, source_target_pairs={{1,33},{2,67},{5,37},{6,71},{9,41},{10,75},{13,45},{14,79},{17,49}... | collective-permute-start | bytes 884744 | tf_op jit(solution)/shard_map/high_up/ppermute | solution.py:35
  76.3 7.5 %collective-permute-start.6 = (bf16[160,1024]{1,0:T(8,128)(2,1)S(1)}, bf16[160,1024]{1,0:T(8,128)(2,1)S(1)}, u32[]{:S(2)}, u32[]{:S(2)}) collective-permute-start(bf16[160,1024]{1,0:T(8,128)(2,1)S(1)} %add_convert_fusion.3), channel_id=1, source_target_pairs={{1,32},{2,66},{5,36},{6,70},{9,40},{10,74},{13,44},{14,78},{17,48}... | collective-permute-start | bytes 983048 | tf_op jit(solution)/shard_map/low_up/ppermute | solution.py:35
  79.9 4.0 %collective-permute-start.7 = (bf16[160,1024]{1,0:T(8,128)(2,1)S(1)}, bf16[160,1024]{1,0:T(8,128)(2,1)S(1)}, u32[]{:S(2)}, u32[]{:S(2)}) collective-permute-start(bf16[160,1024]{1,0:T(8,128)(2,1)S(1)} %add_convert_fusion.3), channel_id=1, source_target_pairs={{3,226},{7,230},{11,234},{15,238},{19,242},{23,246},{27,250},{31,2... | collective-permute-start | bytes 983048 | tf_op jit(solution)/shard_map/low_down/ppermute | solution.py:35
  80.6 8.3 %collective-permute-start.12 = (bf16[160,1024]{1,0:T(8,128)(2,1)S(1)}, bf16[160,1024]{1,0:T(8,128)(2,1)S(1)}, u32[]{:S(2)}, u32[]{:S(2)}) collective-permute-start(bf16[160,1024]{1,0:T(8,128)(2,1)S(1)} %add_convert_fusion.4), channel_id=1, source_target_pairs={{0,2},{1,3},{2,0},{3,1},{4,6},{5,7},{6,4},{7,5},{8,10},{9,11},{10,... | collective-permute-start | bytes 983048 | tf_op jit(solution)/shard_map/row_across/ppermute | solution.py:35
  84.1 11.0 %collective-permute-start.11 = (bf16[160,1024]{1,0:T(8,128)(2,1)S(1)}, bf16[160,1024]{1,0:T(8,128)(2,1)S(1)}, u32[]{:S(2)}, u32[]{:S(2)}) collective-permute-start(bf16[160,1024]{1,0:T(8,128)(2,1)S(1)} %fusion.12), channel_id=1, source_target_pairs={{0,2},{1,3},{2,0},{3,1},{4,6},{5,7},{6,4},{7,5},{8,10},{9,11},{10,... | collective-permute-start | bytes 983048 | tf_op jit(solution)/shard_map/col_across/ppermute | solution.py:35
  95.2 1.8 %copy-start.1 = (bf16[1024,300]{0,1:T(8,128)(2,1)S(1)}, bf16[1024,300]{0,1:T(8,128)(2,1)}, u32[]{:S(2)}) copy-start(bf16[1024,300]{0,1:T(8,128)(2,1)} %param.10) | copy-start | bytes 1843204
  95.2 1.8 %copy-start.2 = (f32[1024,300]{0,1:T(8,128)S(1)}, f32[1024,300]{0,1:T(8,128)}, u32[]{:S(2)}) copy-start(f32[1024,300]{0,1:T(8,128)} %param.12) | copy-start | bytes 3686404
  95.2 1.7 %collective-permute-start.14 = (bf16[160,1024]{1,0:T(8,128)(2,1)S(1)}, bf16[160,1024]{1,0:T(8,128)(2,1)S(1)}, u32[]{:S(2)}, u32[]{:S(2)}) collective-permute-start(bf16[160,1024]{1,0:T(8,128)(2,1)S(1)} %add_convert_fusion), channel_id=1, source_target_pairs={{0,1},{1,0},{2,3},{3,2},{4,5},{5,4},{6,7},{7,6},{8,9},{9,8},{10,11... | collective-permute-start | bytes 983048 | tf_op jit(solution)/shard_map/col_other/ppermute | solution.py:35
  95.7 2.6 %collective-permute-start.13 = (bf16[160,1024]{1,0:T(8,128)(2,1)S(1)}, bf16[160,1024]{1,0:T(8,128)(2,1)S(1)}, u32[]{:S(2)}, u32[]{:S(2)}) collective-permute-start(bf16[160,1024]{1,0:T(8,128)(2,1)S(1)} %add_convert_fusion.1), channel_id=1, source_target_pairs={{0,1},{1,0},{2,3},{3,2},{4,5},{5,4},{6,7},{7,6},{8,9},{9,8},{10,11... | collective-permute-start | bytes 983048 | tf_op jit(solution)/shard_map/row_other/ppermute | solution.py:35
  98.3 1.3 %copy-start.3 = (f32[1024,300]{0,1:T(8,128)S(1)}, f32[1024,300]{0,1:T(8,128)}, u32[]{:S(2)}) copy-start(f32[1024,300]{0,1:T(8,128)} %param.11) | copy-start | bytes 3686404
  98.3 1.4 %copy-start.4 = (bf16[1024,300]{0,1:T(8,128)(2,1)S(1)}, bf16[1024,300]{0,1:T(8,128)(2,1)}, u32[]{:S(2)}) copy-start(bf16[1024,300]{0,1:T(8,128)(2,1)} %param.9) | copy-start | bytes 1843204

commit v2 on v1

--- a/solution.py
+++ b/solution.py
@@ -235,10 +235,8 @@
     )(swap, *args)
 
 
-def adagrad(core, mine, other, table, acc):
-    low = jnp.where(core == 0, mine, other)
-    high = jnp.where(core == 0, other, mine)[: DIM - LOW]
-    total = jnp.concatenate([low, high]).astype(F32)
+def adagrad(low, high, table, acc):
+    total = jnp.concatenate([low, high[: DIM - LOW]]).astype(F32)
     step = LEARN_RATE * total * lax.rsqrt(acc + total * total)
     return (table.astype(F32) - step).astype(BF16)
 
@@ -286,25 +284,29 @@
     high = hop("high", high, way)
     row_keep, row_give = halves(core, row_low, row_high)
     row_chip = add(row_keep, hop("row_swap", row_give, CORE))
-    low, row_chip = barrier((low, row_chip))
+    row_across = hop("row_across", row_chip, ACROSS)
+    high, row_across = barrier((add(grad_1[LOW:], high), row_across))
     low = add(grad_1[:LOW], low)
     low_up = hop("low_up", low, [None, (1, 0), (2, 2), None])
     low_down = hop("low_down", low, [None, None, None, (-1, 2)])
-    high = add(grad_1[LOW:], high)
-    high_up = hop("high_up", high, [None, (1, 1), (2, 3), None])
-    high_down = hop("high_down", high, [(0, 1), None, None, (-1, 3)])
-    low = add(low_up, low_down, jnp.where(is_0, low, 0))
-    high = jnp.pad(add(high_up, high_down), ((0, LOW - HIGH), (0, 0)))
-    col_chip = halves(core, low, high)[0]
-    col_across = hop("col_across", col_chip, ACROSS)
-    row_across = hop("row_across", row_chip, ACROSS)
-    col_across, row_across = barrier((col_across, row_across))
+    high_up = hop("high_up", high, [None, (1, 0), (2, 3), None])
+    high_down = hop("high_down", high, [None, None, None, (-1, 3)])
+    high = add(high_up, high_down, jnp.where(is_0, high, 0))
+    high_across = hop("high_across", high, [(0, 3), None, None, (0, 0)])
+    high = add(high, high_across)
+    high = high + hop("high_other", high, [(0, 1), None, None, (0, 2)])
+    low_up, row_across = barrier((low_up, row_across))
     row_mine = add(row_chip, row_across)
     row_other = hop("row_other", row_mine, CORE)
-    new_row = adagrad(core, row_mine, row_other, row_emb.T, row_acc.T)
-    col_mine = add(col_chip, col_across)
-    col_other = hop("col_other", col_mine, CORE)
-    new_col = adagrad(core, col_mine, col_other, col_emb.T, col_acc.T)
+    row_low, row_high = halves(core, row_mine, row_other)
+    new_row = adagrad(row_low, row_high, row_emb.T, row_acc.T)
+
+    low = add(low_up, low_down, jnp.where(is_0, low, 0))
+    low_across = hop("low_across", low, [(0, 2), None, (0, 0), None])
+    low_across, new_row = barrier((low_across, new_row))
+    low = add(low, low_across)
+    low = low + hop("low_other", low, [(0, 1), None, (0, 3), None])
+    new_col = adagrad(low, high, col_emb.T, col_acc.T)
     return (new_row.T, new_col.T)
 
 

time: 102 us -> 100 us (0.980)
  starting transfers between devices: 32 us -> 34 us
  waiting for transfers between devices: 40.5 us -> 38.5 us
  local copies, waits for them, and re-layouts: 1.39 us -> 0.04 us
    ppermute x15 -> x17, waiting for transfers between devices: 40.5 us -> 38.5 us  [hop(): return lax.ppermute(array, AXES, perm)]
    ppermute x15 -> x17, starting transfers between devices: 32 us -> 34 us  [hop(): return lax.ppermute(array, AXES, perm)]
    unnamed x12, local copies, waits for them, and re-layouts: 1.39 us -> 0.04 us
    convert_element_type x0 -> x1, other arithmetic: none -> 1.2 us  [adagrad(): return (table.astype(F32) - step).astype(BF16)]
    transpose x2 -> x1, other arithmetic: 2.4 us -> 1.2 us  [per_device(): return (new_row.T, new_col.T)]
  transfers between devices with their start and end apart: 15 -> 17, of which waited for: 9 -> 8; matrix products, arithmetic and copies ran while one was open for 2% -> 2% of each run, Pallas kernels for 12% -> 12%
where the time goes in v2:
time: 100 us; the launch traced here: 99.7 us
  waiting for transfers between devices  38.5 us (38%)
  starting transfers between devices  34 us (34%)
  Pallas kernels  22.7 us (23%)
  other arithmetic  3.56 us (4%)
    ppermute x17, waiting for transfers between devices, hop(): return lax.ppermute(array, AXES, perm)  38.5 us
    ppermute x17, starting transfers between devices, hop(): return lax.ppermute(array, AXES, perm)  34 us
    pallas_call x1, Pallas kernels, second_pair(): pl.pallas_call(second_kernel, out_shape=(vmem(LOW), vmem(HIGH), shape(LOW...  8.71 us
    pallas_call x1, Pallas kernels, first_pair(): pl.pallas_call(first_kernel, out_shape=(vmem(WIDE), pltpu.HBM((WIDE, TERM...  8.53 us
    pallas_call x1, Pallas kernels, pick_rows(): pl.pallas_call(rows_kernel, out_shape=(shape(WIDE), shape(WIDE)), in_spec...  3.44 us
  transfers between devices with their start and end apart: 17, of which 8 were waited for; matrix products, arithmetic and copies ran while one was open for 2% of the time, Pallas kernels for 12%

profile of v2, /device:TPU:1, one launch (start us, length us, event | category | flops | bytes accessed | tf_op | source)
XLA Modules:
  0.0 99.7 jit_solution(6290481182601433008)
XLA Ops:
  0.6 2.0 %shard_map.104 = (bf16[304,1024]{1,0:T(8,128)(2,1)}, s32[1,1024]{1,0:T(1,128)}) custom-call(s32[1]{0:T(128)} %bitcast.swap_ref, bf16[300,1024]{1,0:T(8,128)(2,1)} %bitcast.15, bf16[1024]{0:T(1024)(128)(2,1)} %off_ref.2, s32[1,1,2,1024]{3,2,1,0:T(2,128)} %idx_ref.2), custom_call_target="tpu_custom_call" | custom-call | bytes 1300000 | tf_op jit(solution)/shard_map/pallas_call | solution.py:98
  2.6 8.3 %collective-permute-start = (bf16[304,1024]{1,0:T(8,128)(2,1)}, bf16[304,1024]{1,0:T(8,128)(2,1)S(1)}, u32[]{:S(2)}, u32[]{:S(2)}) collective-permute-start(bf16[304,1024]{1,0:T(8,128)(2,1)} %get-tuple-element.24), channel_id=1, source_target_pairs={{0,0},{1,225},{2,194},{3,35},{4,4},{5,229},{6,198},{7,39},{8,8},{9... | collective-permute-start | bytes 1867784 | tf_op jit(solution)/shard_map/got/ppermute | solution.py:35
  10.9 1.9 %collective-permute-start.2 = (bf16[304,1024]{1,0:T(8,128)(2,1)}, bf16[304,1024]{1,0:T(8,128)(2,1)S(1)}, u32[]{:S(2)}, u32[]{:S(2)}) collective-permute-start(bf16[304,1024]{1,0:T(8,128)(2,1)} %get-tuple-element.24), channel_id=1, source_target_pairs={{1,97},{5,101},{9,105},{13,109},{17,113},{21,117},{25,121},{29,125... | collective-permute-start | bytes 1867784 | tf_op jit(solution)/shard_map/far/ppermute | solution.py:35
  12.9 3.4 %shard_map.105 = (bf16[304,1024]{1,0:T(8,128)(2,1)}, bf16[304,1024]{1,0:T(8,128)(2,1)}) custom-call(s32[1]{0:T(128)} %bitcast.swap_ref, bf16[300,1024]{1,0:T(8,128)(2,1)} %bitcast.16, bf16[1024]{0:T(1024)(128)(2,1)} %off_ref.3, s32[1,1,2,1024]{3,2,1,0:T(2,128)} %row_idx_ref.3), custom_call_target="tpu_custom_call" | custom-call | flops 1275068416 | bytes 2000000 | tf_op jit(solution)/shard_map/pallas_call | solution.py:118
  16.3 2.1 %collective-permute-done.block_ref = bf16[304,1024]{1,0:T(8,128)(2,1)S(1)} collective-permute-done((bf16[304,1024]{1,0:T(8,128)(2,1)}, bf16[304,1024]{1,0:T(8,128)(2,1)S(1)}, u32[]{:S(2)}, u32[]{:S(2)}) %collective-permute-start) | collective-permute-done | bytes 622624 | tf_op jit(solution)/shard_map/got/ppermute | solution.py:35
  18.4 1.3 %collective-permute-start.1 = (bf16[304,1024]{1,0:T(8,128)(2,1)S(1)}, bf16[304,1024]{1,0:T(8,128)(2,1)S(1)}, u32[]{:S(2)}, u32[]{:S(2)}) collective-permute-start(bf16[304,1024]{1,0:T(8,128)(2,1)S(1)} %collective-permute-done.block_ref), channel_id=1, source_target_pairs={{1,160},{2,227},{3,34},{5,164},{6,231},{7,38},{9,168},{10,235},{11... | collective-permute-start | bytes 1867784 | tf_op jit(solution)/shard_map/near/ppermute | solution.py:35
  19.7 2.2 %collective-permute-start.3 = (s32[1,1024]{1,0:T(1,128)S(1)}, s32[1,1024]{1,0:T(1,128)S(1)}, u32[]{:S(2)}, u32[]{:S(2)}) collective-permute-start(s32[1,1024]{1,0:T(1,128)S(1)} %copy-done.5), channel_id=1, source_target_pairs={{0,128},{1,97},{2,66},{3,163},{4,132},{5,101},{6,70},{7,167},{8,13... | collective-permute-start | bytes 12296 | tf_op jit(solution)/shard_map/idx_2/ppermute | solution.py:35
  22.0 8.5 %shard_map.106 = (bf16[304,1024]{1,0:T(8,128)(2,1)S(1)}, f32[304,1024]{1,0:T(8,128)}) custom-call(s32[1]{0:T(128)} %bitcast.swap_ref, s32[2,1024,1024]{2,1,0:T(8,128)} %bitcast.18, bf16[304,1024]{1,0:T(8,128)(2,1)} %get-tuple-element.28.row_ref, s32[1,1,2,1024]{3,2,1,0:T(2,128)S(1)} %copy-done, bf16[304,1024]{1,0:T(8,128)(2,1)S(1)} %collective-permute-done.block_ref), custom_call_target="tpu_custom_call" | custom-call | flops 3825205248 | bytes 12000000 | tf_op jit(solution)/shard_map/pallas_call | solution.py:192
  30.5 6.2 %collective-permute-done.3.idx_ref = s32[1,1024]{1,0:T(1,128)S(1)} collective-permute-done((s32[1,1024]{1,0:T(1,128)S(1)}, s32[1,1024]{1,0:T(1,128)S(1)}, u32[]{:S(2)}, u32[]{:S(2)}) %collective-permute-start.3) | collective-permute-done | bytes 4128 | tf_op jit(solution)/shard_map/idx_2/ppermute | solution.py:35
  36.7 2.6 %collective-permute-done.1.block_2_ref = bf16[304,1024]{1,0:T(8,128)(2,1)S(1)} collective-permute-done((bf16[304,1024]{1,0:T(8,128)(2,1)S(1)}, bf16[304,1024]{1,0:T(8,128)(2,1)S(1)}, u32[]{:S(2)}, u32[]{:S(2)}) %collective-permute-start.1) | collective-permute-done | bytes 622624 | tf_op jit(solution)/shard_map/near/ppermute | solution.py:35
  39.3 8.7 %shard_map.107 = (bf16[160,1024]{1,0:T(8,128)(2,1)S(1)}, bf16[144,1024]{1,0:T(8,128)(2,1)S(1)}, bf16[160,1024]{1,0:T(8,128)(2,1)S(1)}, bf16[160,1024]{1,0:T(8,128)(2,1)S(1)}) custom-call(s32[1]{0:T(128)} %bitcast.swap_ref, s32[2,1024,1024]{2,1,0:T(8,128)} %bitcast.19, bf16[304,1024]{1,0:T(8,128)(2,1)} %get-tuple-element.31.row_ref, ...), custom_call_target="tpu_custom_call" | custom-call | flops 3825205248 | bytes 12000000 | tf_op jit(solution)/shard_map/pallas_call | solution.py:227
  48.1 2.8 %collective-permute-start.7 = (bf16[160,1024]{1,0:T(8,128)(2,1)S(1)}, bf16[160,1024]{1,0:T(8,128)(2,1)S(1)}, u32[]{:S(2)}, u32[]{:S(2)}) collective-permute-start(bf16[160,1024]{1,0:T(8,128)(2,1)S(1)} %broadcast_select_fusion.1), channel_id=1, source_target_pairs={{0,1},{1,0},{2,3},{3,2},{4,5},{5,4},{6,7},{7,6},{8,9},{9,8},{10,11... | collective-permute-start | bytes 983048 | tf_op jit(solution)/shard_map/row_swap/ppermute | solution.py:35
  50.9 2.9 %collective-permute-start.4 = (bf16[160,1024]{1,0:T(8,128)(2,1)S(1)}, bf16[160,1024]{1,0:T(8,128)(2,1)S(1)}, u32[]{:S(2)}, u32[]{:S(2)}) collective-permute-start(bf16[160,1024]{1,0:T(8,128)(2,1)S(1)} %get-tuple-element.36), channel_id=1, source_target_pairs={{0,97},{1,160},{2,227},{3,34},{4,101},{5,164},{6,231},{7,38},{8,10... | collective-permute-start | bytes 983048 | tf_op jit(solution)/shard_map/low/ppermute | solution.py:35
  53.8 1.9 %collective-permute-start.6 = (bf16[144,1024]{1,0:T(8,128)(2,1)S(1)}, bf16[144,1024]{1,0:T(8,128)(2,1)S(1)}, u32[]{:S(2)}, u32[]{:S(2)}) collective-permute-start(bf16[144,1024]{1,0:T(8,128)(2,1)S(1)} %get-tuple-element.37), channel_id=1, source_target_pairs={{0,97},{1,160},{2,227},{3,34},{4,101},{5,164},{6,231},{7,38},{8,10... | collective-permute-start | bytes 884744 | tf_op jit(solution)/shard_map/high/ppermute | solution.py:35
  56.9 14.5 %collective-permute-done.4 = bf16[160,1024]{1,0:T(8,128)(2,1)S(1)} collective-permute-done((bf16[160,1024]{1,0:T(8,128)(2,1)S(1)}, bf16[160,1024]{1,0:T(8,128)(2,1)S(1)}, u32[]{:S(2)}, u32[]{:S(2)}) %collective-permute-start.4) | collective-permute-done | bytes 327712 | tf_op jit(solution)/shard_map/low/ppermute | solution.py:35
  71.5 1.3 %collective-permute-start.5 = (bf16[160,1024]{1,0:T(8,128)(2,1)S(1)}, bf16[160,1024]{1,0:T(8,128)(2,1)S(1)}, u32[]{:S(2)}, u32[]{:S(2)}) collective-permute-start(bf16[160,1024]{1,0:T(8,128)(2,1)S(1)} %add_convert_fusion.4), channel_id=1, source_target_pairs={{1,32},{2,66},{5,36},{6,70},{9,40},{10,74},{13,44},{14,78},{17,48}... | collective-permute-start | bytes 983048 | tf_op jit(solution)/shard_map/low_up/ppermute | solution.py:35
  73.5 3.0 %collective-permute-done.6 = bf16[144,1024]{1,0:T(8,128)(2,1)S(1)} collective-permute-done((bf16[144,1024]{1,0:T(8,128)(2,1)S(1)}, bf16[144,1024]{1,0:T(8,128)(2,1)S(1)}, u32[]{:S(2)}, u32[]{:S(2)}) %collective-permute-start.6) | collective-permute-done | bytes 294944 | tf_op jit(solution)/shard_map/high/ppermute | solution.py:35
  76.6 3.7 %collective-permute-start.13 = (bf16[144,1024]{1,0:T(8,128)(2,1)S(1)}, bf16[144,1024]{1,0:T(8,128)(2,1)S(1)}, u32[]{:S(2)}, u32[]{:S(2)}) collective-permute-start(bf16[144,1024]{1,0:T(8,128)(2,1)S(1)} %add_convert_fusion.7), channel_id=1, source_target_pairs={{1,32},{2,67},{5,36},{6,71},{9,40},{10,75},{13,44},{14,79},{17,48}... | collective-permute-start | bytes 884744 | tf_op jit(solution)/shard_map/high_up/ppermute | solution.py:35
  84.8 1.2 %fusion.2 = bf16[300,1024]{1,0:T(8,128)(2,1)} fusion(f32[1024,300]{0,1:T(8,128)S(1)} %copy-done.2, bf16[140,1024]{1,0:T(8,128)(2,1)S(1)} %slice_select_fusion, bf16[160,1024]{1,0:T(8,128)(2,1)S(1)} %broadcast_select_fusion, bf16[1024,300]{0,1:T(8,128)(2,1)S(1)} %copy-done.4), kind=kLoop, calls=%fused_computation.6 | loop fusion | flops 3379200 | bytes 3072000 | tf_op jit(solution)/shard_map/convert_element_type | solution.py:241
  86.2 1.4 %collective-permute-start.12 = (bf16[160,1024]{1,0:T(8,128)(2,1)S(1)}, bf16[160,1024]{1,0:T(8,128)(2,1)S(1)}, u32[]{:S(2)}, u32[]{:S(2)}) collective-permute-start(bf16[160,1024]{1,0:T(8,128)(2,1)S(1)} %add_convert_fusion), channel_id=1, source_target_pairs={{0,1},{2,3},{4,5},{6,7},{8,9},{10,11},{12,13},{14,15},{16,17},{18,... | collective-permute-start | bytes 983048 | tf_op jit(solution)/shard_map/low_other/ppermute | solution.py:35
  87.7 1.3 %collective-permute-start.16 = (bf16[144,1024]{1,0:T(8,128)(2,1)S(1)}, bf16[144,1024]{1,0:T(8,128)(2,1)S(1)}, u32[]{:S(2)}, u32[]{:S(2)}) collective-permute-start(bf16[144,1024]{1,0:T(8,128)(2,1)S(1)} %add_convert_fusion.5), channel_id=1, source_target_pairs={{0,1},{3,2},{4,5},{7,6},{8,9},{11,10},{12,13},{15,14},{16,17},{19,... | collective-permute-start | bytes 884744 | tf_op jit(solution)/shard_map/high_other/ppermute | solution.py:35
  89.0 7.8 %collective-permute-done.12 = bf16[160,1024]{1,0:T(8,128)(2,1)S(1)} collective-permute-done((bf16[160,1024]{1,0:T(8,128)(2,1)S(1)}, bf16[160,1024]{1,0:T(8,128)(2,1)S(1)}, u32[]{:S(2)}, u32[]{:S(2)}) %collective-permute-start.12) | collective-permute-done | bytes 327712 | tf_op jit(solution)/shard_map/low_other/ppermute | solution.py:35
  96.9 1.6 %collective-permute-done.16 = bf16[144,1024]{1,0:T(8,128)(2,1)S(1)} collective-permute-done((bf16[144,1024]{1,0:T(8,128)(2,1)S(1)}, bf16[144,1024]{1,0:T(8,128)(2,1)S(1)}, u32[]{:S(2)}, u32[]{:S(2)}) %collective-permute-start.16) | collective-permute-done | bytes 294944 | tf_op jit(solution)/shard_map/high_other/ppermute | solution.py:35
  98.5 1.2 %fusion.10 = bf16[1024,300]{0,1:T(8,128)(2,1)} fusion(f32[1024,300]{0,1:T(8,128)S(1)} %copy-done.3, bf16[140,1024]{1,0:T(8,128)(2,1)S(1)} %slice_add_fusion, bf16[160,1024]{1,0:T(8,128)(2,1)S(1)} %add.50, bf16[1024,300]{0,1:T(8,128)(2,1)S(1)} %copy-done.1), kind=kLoop, calls=%fused_computation.19 | loop fusion | flops 3379200 | bytes 3072000 | tf_op jit(solution)/shard_map/transpose | solution.py:310
  (41 shorter events, 7.0 us)
Async XLA Ops:
  2.6 15.8 %collective-permute-start = (bf16[304,1024]{1,0:T(8,128)(2,1)}, bf16[304,1024]{1,0:T(8,128)(2,1)S(1)}, u32[]{:S(2)}, u32[]{:S(2)}) collective-permute-start(bf16[304,1024]{1,0:T(8,128)(2,1)} %get-tuple-element.24), channel_id=1, source_target_pairs={{0,0},{1,225},{2,194},{3,35},{4,4},{5,229},{6,198},{7,39},{8,8},{9... | collective-permute-start | bytes 1867784 | tf_op jit(solution)/shard_map/got/ppermute | solution.py:35
  10.9 25.8 %collective-permute-start.2 = (bf16[304,1024]{1,0:T(8,128)(2,1)}, bf16[304,1024]{1,0:T(8,128)(2,1)S(1)}, u32[]{:S(2)}, u32[]{:S(2)}) collective-permute-start(bf16[304,1024]{1,0:T(8,128)(2,1)} %get-tuple-element.24), channel_id=1, source_target_pairs={{1,97},{5,101},{9,105},{13,109},{17,113},{21,117},{25,121},{29,125... | collective-permute-start | bytes 1867784 | tf_op jit(solution)/shard_map/far/ppermute | solution.py:35
  12.9 6.9 %copy-start.5 = (s32[1,1024]{1,0:T(1,128)S(1)}, s32[1,1024]{1,0:T(1,128)}, u32[]{:S(2)}) copy-start(s32[1,1024]{1,0:T(1,128)} %get-tuple-element.27) | copy-start | bytes 12292
  12.9 9.1 %copy-start = (s32[1,1,2,1024]{3,2,1,0:T(2,128)S(1)}, s32[1,1,2,1024]{3,2,1,0:T(2,128)}, u32[]{:S(2)}) copy-start(s32[1,1,2,1024]{3,2,1,0:T(2,128)} %row_idx_ref.3) | copy-start | bytes 24580
  18.4 20.9 %collective-permute-start.1 = (bf16[304,1024]{1,0:T(8,128)(2,1)S(1)}, bf16[304,1024]{1,0:T(8,128)(2,1)S(1)}, u32[]{:S(2)}, u32[]{:S(2)}) collective-permute-start(bf16[304,1024]{1,0:T(8,128)(2,1)S(1)} %collective-permute-done.block_ref), channel_id=1, source_target_pairs={{1,160},{2,227},{3,34},{5,164},{6,231},{7,38},{9,168},{10,235},{11... | collective-permute-start | bytes 1867784 | tf_op jit(solution)/shard_map/near/ppermute | solution.py:35
  19.7 17.0 %collective-permute-start.3 = (s32[1,1024]{1,0:T(1,128)S(1)}, s32[1,1024]{1,0:T(1,128)S(1)}, u32[]{:S(2)}, u32[]{:S(2)}) collective-permute-start(s32[1,1024]{1,0:T(1,128)S(1)} %copy-done.5), channel_id=1, source_target_pairs={{0,128},{1,97},{2,66},{3,163},{4,132},{5,101},{6,70},{7,167},{8,13... | collective-permute-start | bytes 12296 | tf_op jit(solution)/shard_map/idx_2/ppermute | solution.py:35
  48.1 7.6 %collective-permute-start.7 = (bf16[160,1024]{1,0:T(8,128)(2,1)S(1)}, bf16[160,1024]{1,0:T(8,128)(2,1)S(1)}, u32[]{:S(2)}, u32[]{:S(2)}) collective-permute-start(bf16[160,1024]{1,0:T(8,128)(2,1)S(1)} %broadcast_select_fusion.1), channel_id=1, source_target_pairs={{0,1},{1,0},{2,3},{3,2},{4,5},{5,4},{6,7},{7,6},{8,9},{9,8},{10,11... | collective-permute-start | bytes 983048 | tf_op jit(solution)/shard_map/row_swap/ppermute | solution.py:35
  50.9 20.5 %collective-permute-start.4 = (bf16[160,1024]{1,0:T(8,128)(2,1)S(1)}, bf16[160,1024]{1,0:T(8,128)(2,1)S(1)}, u32[]{:S(2)}, u32[]{:S(2)}) collective-permute-start(bf16[160,1024]{1,0:T(8,128)(2,1)S(1)} %get-tuple-element.36), channel_id=1, source_target_pairs={{0,97},{1,160},{2,227},{3,34},{4,101},{5,164},{6,231},{7,38},{8,10... | collective-permute-start | bytes 983048 | tf_op jit(solution)/shard_map/low/ppermute | solution.py:35
  53.8 22.7 %collective-permute-start.6 = (bf16[144,1024]{1,0:T(8,128)(2,1)S(1)}, bf16[144,1024]{1,0:T(8,128)(2,1)S(1)}, u32[]{:S(2)}, u32[]{:S(2)}) collective-permute-start(bf16[144,1024]{1,0:T(8,128)(2,1)S(1)} %get-tuple-element.37), channel_id=1, source_target_pairs={{0,97},{1,160},{2,227},{3,34},{4,101},{5,164},{6,231},{7,38},{8,10... | collective-permute-start | bytes 884744 | tf_op jit(solution)/shard_map/high/ppermute | solution.py:35
  55.9 20.7 %collective-permute-start.8 = (bf16[160,1024]{1,0:T(8,128)(2,1)S(1)}, bf16[160,1024]{1,0:T(8,128)(2,1)S(1)}, u32[]{:S(2)}, u32[]{:S(2)}) collective-permute-start(bf16[160,1024]{1,0:T(8,128)(2,1)S(1)} %add_convert_fusion.3), channel_id=1, source_target_pairs={{0,2},{1,3},{2,0},{3,1},{4,6},{5,7},{6,4},{7,5},{8,10},{9,11},{10,... | collective-permute-start | bytes 983048 | tf_op jit(solution)/shard_map/row_across/ppermute | solution.py:35
  71.5 9.4 %collective-permute-start.5 = (bf16[160,1024]{1,0:T(8,128)(2,1)S(1)}, bf16[160,1024]{1,0:T(8,128)(2,1)S(1)}, u32[]{:S(2)}, u32[]{:S(2)}) collective-permute-start(bf16[160,1024]{1,0:T(8,128)(2,1)S(1)} %add_convert_fusion.4), channel_id=1, source_target_pairs={{1,32},{2,66},{5,36},{6,70},{9,40},{10,74},{13,44},{14,78},{17,48}... | collective-permute-start | bytes 983048 | tf_op jit(solution)/shard_map/low_up/ppermute | solution.py:35
  72.8 9.2 %collective-permute-start.9 = (bf16[160,1024]{1,0:T(8,128)(2,1)S(1)}, bf16[160,1024]{1,0:T(8,128)(2,1)S(1)}, u32[]{:S(2)}, u32[]{:S(2)}) collective-permute-start(bf16[160,1024]{1,0:T(8,128)(2,1)S(1)} %add_convert_fusion.4), channel_id=1, source_target_pairs={{3,226},{7,230},{11,234},{15,238},{19,242},{23,246},{27,250},{31,2... | collective-permute-start | bytes 983048 | tf_op jit(solution)/shard_map/low_down/ppermute | solution.py:35
  76.6 7.3 %collective-permute-start.13 = (bf16[144,1024]{1,0:T(8,128)(2,1)S(1)}, bf16[144,1024]{1,0:T(8,128)(2,1)S(1)}, u32[]{:S(2)}, u32[]{:S(2)}) collective-permute-start(bf16[144,1024]{1,0:T(8,128)(2,1)S(1)} %add_convert_fusion.7), channel_id=1, source_target_pairs={{1,32},{2,67},{5,36},{6,71},{9,40},{10,75},{13,44},{14,79},{17,48}... | collective-permute-start | bytes 884744 | tf_op jit(solution)/shard_map/high_up/ppermute | solution.py:35
  80.2 3.6 %collective-permute-start.14 = (bf16[144,1024]{1,0:T(8,128)(2,1)S(1)}, bf16[144,1024]{1,0:T(8,128)(2,1)S(1)}, u32[]{:S(2)}, u32[]{:S(2)}) collective-permute-start(bf16[144,1024]{1,0:T(8,128)(2,1)S(1)} %add_convert_fusion.7), channel_id=1, source_target_pairs={{3,227},{7,231},{11,235},{15,239},{19,243},{23,247},{27,251},{31,2... | collective-permute-start | bytes 884744 | tf_op jit(solution)/shard_map/high_down/ppermute | solution.py:35
  81.0 3.7 %collective-permute-start.11 = (bf16[160,1024]{1,0:T(8,128)(2,1)S(1)}, bf16[160,1024]{1,0:T(8,128)(2,1)S(1)}, u32[]{:S(2)}, u32[]{:S(2)}) collective-permute-start(bf16[160,1024]{1,0:T(8,128)(2,1)S(1)} %add_convert_fusion.1), channel_id=1, source_target_pairs={{0,1},{1,0},{2,3},{3,2},{4,5},{5,4},{6,7},{7,6},{8,9},{9,8},{10,11... | collective-permute-start | bytes 983048 | tf_op jit(solution)/shard_map/row_other/ppermute | solution.py:35
  82.2 2.6 %copy-start.2 = (f32[1024,300]{0,1:T(8,128)S(1)}, f32[1024,300]{0,1:T(8,128)}, u32[]{:S(2)}) copy-start(f32[1024,300]{0,1:T(8,128)} %param.11) | copy-start | bytes 3686404
  82.2 2.6 %copy-start.4 = (bf16[1024,300]{0,1:T(8,128)(2,1)S(1)}, bf16[1024,300]{0,1:T(8,128)(2,1)}, u32[]{:S(2)}) copy-start(bf16[1024,300]{0,1:T(8,128)(2,1)} %param.9) | copy-start | bytes 1843204
  82.2 3.8 %collective-permute-start.10 = (bf16[160,1024]{1,0:T(8,128)(2,1)S(1)}, bf16[160,1024]{1,0:T(8,128)(2,1)S(1)}, u32[]{:S(2)}, u32[]{:S(2)}) collective-permute-start(bf16[160,1024]{1,0:T(8,128)(2,1)S(1)} %add_convert_fusion.2), channel_id=1, source_target_pairs={{0,2},{2,0},{4,6},{6,4},{8,10},{10,8},{12,14},{14,12},{16,18},{18,... | collective-permute-start | bytes 983048 | tf_op jit(solution)/shard_map/low_across/ppermute | solution.py:35
  84.0 3.6 %collective-permute-start.15 = (bf16[144,1024]{1,0:T(8,128)(2,1)S(1)}, bf16[144,1024]{1,0:T(8,128)(2,1)S(1)}, u32[]{:S(2)}, u32[]{:S(2)}) collective-permute-start(bf16[144,1024]{1,0:T(8,128)(2,1)S(1)} %add_convert_fusion.6), channel_id=1, source_target_pairs={{0,3},{3,0},{4,7},{7,4},{8,11},{11,8},{12,15},{15,12},{16,19},{19,... | collective-permute-start | bytes 884744 | tf_op jit(solution)/shard_map/high_across/ppermute | solution.py:35
  86.2 12.3 %copy-start.1 = (bf16[1024,300]{0,1:T(8,128)(2,1)S(1)}, bf16[1024,300]{0,1:T(8,128)(2,1)}, u32[]{:S(2)}) copy-start(bf16[1024,300]{0,1:T(8,128)(2,1)} %param.10) | copy-start | bytes 1843204
  86.2 12.3 %copy-start.3 = (f32[1024,300]{0,1:T(8,128)S(1)}, f32[1024,300]{0,1:T(8,128)}, u32[]{:S(2)}) copy-start(f32[1024,300]{0,1:T(8,128)} %param.12) | copy-start | bytes 3686404
  86.2 10.6 %collective-permute-start.12 = (bf16[160,1024]{1,0:T(8,128)(2,1)S(1)}, bf16[160,1024]{1,0:T(8,128)(2,1)S(1)}, u32[]{:S(2)}, u32[]{:S(2)}) collective-permute-start(bf16[160,1024]{1,0:T(8,128)(2,1)S(1)} %add_convert_fusion), channel_id=1, source_target_pairs={{0,1},{2,3},{4,5},{6,7},{8,9},{10,11},{12,13},{14,15},{16,17},{18,... | collective-permute-start | bytes 983048 | tf_op jit(solution)/shard_map/low_other/ppermute | solution.py:35
  87.7 10.8 %collective-permute-start.16 = (bf16[144,1024]{1,0:T(8,128)(2,1)S(1)}, bf16[144,1024]{1,0:T(8,128)(2,1)S(1)}, u32[]{:S(2)}, u32[]{:S(2)}) collective-permute-start(bf16[144,1024]{1,0:T(8,128)(2,1)S(1)} %add_convert_fusion.5), channel_id=1, source_target_pairs={{0,1},{3,2},{4,5},{7,6},{8,9},{11,10},{12,13},{15,14},{16,17},{19,... | collective-permute-start | bytes 884744 | tf_op jit(solution)/shard_map/high_other/ppermute | solution.py:35

commit v3 on v2

--- a/solution.py
+++ b/solution.py
@@ -125,18 +125,13 @@
     )(swap, emb, off, idx)
 
 
-def weights(count):
+def cells(score, count):
     scale = 1.0 / TERMS
     count_f = count.astype(F32)
     slope = 0.1 * scale + (0.25 * scale) * (count_f * lax.rsqrt(count_f))
-    base = slope * jnp.log(count_f)
-    return jnp.where(count > 0, slope, 0.0), jnp.where(count > 0, base, 0.0)
-
-
-def cells(score, slope, base):
-    scale = 0.5 / TERMS
-    unseen = scale + scale * jnp.tanh(0.5 * score)
-    return jnp.where(slope > 0, slope * score - base, unseen).astype(BF16)
+    seen = slope * (score - jnp.log(count_f))
+    unseen = 0.5 * scale + (0.5 * scale) * jnp.tanh(0.5 * score)
+    return jnp.where(count > 0, seen, unseen).astype(BF16)
 
 
 def start(src, dst, sem):
@@ -155,7 +150,7 @@
     get_row.wait()
     est = dot(row[...], col, 0, 0)
     get_counts.wait()
-    cell_buf[...] = cells(est, *weights(counts[...]))
+    cell_buf[...] = cells(est, counts[...])
     grad = dot(row[...], cell_buf[...], 1, 0).astype(BF16)
     grad = dot(grad, pick, 1, 1).astype(BF16)
     row_part = dot(col, cell_buf[...], 1, 1).astype(BF16)

time: 100 us -> 99.5 us (level)
  Pallas kernels: 22.7 us -> 21.1 us
  waiting for transfers between devices: 38.5 us -> 39.9 us
    ppermute x17, waiting for transfers between devices: 38.5 us -> 39.9 us  [hop(): return lax.ppermute(array, AXES, perm)]
  transfers between devices with their start and end apart: 17 -> 17, of which waited for: 8 -> 8; matrix products, arithmetic and copies ran while one was open for 2% -> 2% of each run, Pallas kernels for 12% -> 11%
where the time goes in v3:
time: 99.5 us; the launch traced here: 99 us
  waiting for transfers between devices  39.9 us (40%)
  starting transfers between devices  33.4 us (34%)
  Pallas kernels  21.1 us (21%)
  other arithmetic  3.56 us (4%)
    ppermute x17, waiting for transfers between devices, hop(): return lax.ppermute(array, AXES, perm)  39.9 us
    ppermute x17, starting transfers between devices, hop(): return lax.ppermute(array, AXES, perm)  33.4 us
    pallas_call x1, Pallas kernels, first_pair(): pl.pallas_call(first_kernel, out_shape=(vmem(WIDE), pltpu.HBM((WIDE, TERM...  7.86 us
    pallas_call x1, Pallas kernels, second_pair(): pl.pallas_call(second_kernel, out_shape=(vmem(LOW), vmem(HIGH), shape(LOW...  7.83 us
    pallas_call x1, Pallas kernels, pick_rows(): pl.pallas_call(rows_kernel, out_shape=(shape(WIDE), shape(WIDE)), in_spec...  3.44 us
  transfers between devices with their start and end apart: 17, of which 8 were waited for; matrix products, arithmetic and copies ran while one was open for 2% of the time, Pallas kernels for 11%

profile of v3, /device:TPU:1, one launch (start us, length us, event | category | flops | bytes accessed | tf_op | source)
XLA Modules:
  0.0 99.0 jit_solution(12182102965331865908)
XLA Ops:
  0.6 2.0 %shard_map.104 = (bf16[304,1024]{1,0:T(8,128)(2,1)}, s32[1,1024]{1,0:T(1,128)}) custom-call(s32[1]{0:T(128)} %bitcast.swap_ref, bf16[300,1024]{1,0:T(8,128)(2,1)} %bitcast.15, bf16[1024]{0:T(1024)(128)(2,1)} %off_ref.2, s32[1,1,2,1024]{3,2,1,0:T(2,128)} %idx_ref.2), custom_call_target="tpu_custom_call" | custom-call | bytes 1300000 | tf_op jit(solution)/shard_map/pallas_call | solution.py:98
  2.6 8.3 %collective-permute-start = (bf16[304,1024]{1,0:T(8,128)(2,1)}, bf16[304,1024]{1,0:T(8,128)(2,1)S(1)}, u32[]{:S(2)}, u32[]{:S(2)}) collective-permute-start(bf16[304,1024]{1,0:T(8,128)(2,1)} %get-tuple-element.24), channel_id=1, source_target_pairs={{0,0},{1,225},{2,194},{3,35},{4,4},{5,229},{6,198},{7,39},{8,8},{9... | collective-permute-start | bytes 1867784 | tf_op jit(solution)/shard_map/got/ppermute | solution.py:35
  10.9 1.9 %collective-permute-start.2 = (bf16[304,1024]{1,0:T(8,128)(2,1)}, bf16[304,1024]{1,0:T(8,128)(2,1)S(1)}, u32[]{:S(2)}, u32[]{:S(2)}) collective-permute-start(bf16[304,1024]{1,0:T(8,128)(2,1)} %get-tuple-element.24), channel_id=1, source_target_pairs={{1,97},{5,101},{9,105},{13,109},{17,113},{21,117},{25,121},{29,125... | collective-permute-start | bytes 1867784 | tf_op jit(solution)/shard_map/far/ppermute | solution.py:35
  12.9 3.4 %shard_map.105 = (bf16[304,1024]{1,0:T(8,128)(2,1)}, bf16[304,1024]{1,0:T(8,128)(2,1)}) custom-call(s32[1]{0:T(128)} %bitcast.swap_ref, bf16[300,1024]{1,0:T(8,128)(2,1)} %bitcast.16, bf16[1024]{0:T(1024)(128)(2,1)} %off_ref.3, s32[1,1,2,1024]{3,2,1,0:T(2,128)} %row_idx_ref.3), custom_call_target="tpu_custom_call" | custom-call | flops 1275068416 | bytes 2000000 | tf_op jit(solution)/shard_map/pallas_call | solution.py:118
  16.3 2.1 %collective-permute-done.block_ref = bf16[304,1024]{1,0:T(8,128)(2,1)S(1)} collective-permute-done((bf16[304,1024]{1,0:T(8,128)(2,1)}, bf16[304,1024]{1,0:T(8,128)(2,1)S(1)}, u32[]{:S(2)}, u32[]{:S(2)}) %collective-permute-start) | collective-permute-done | bytes 622624 | tf_op jit(solution)/shard_map/got/ppermute | solution.py:35
  18.4 1.3 %collective-permute-start.1 = (bf16[304,1024]{1,0:T(8,128)(2,1)S(1)}, bf16[304,1024]{1,0:T(8,128)(2,1)S(1)}, u32[]{:S(2)}, u32[]{:S(2)}) collective-permute-start(bf16[304,1024]{1,0:T(8,128)(2,1)S(1)} %collective-permute-done.block_ref), channel_id=1, source_target_pairs={{1,160},{2,227},{3,34},{5,164},{6,231},{7,38},{9,168},{10,235},{11... | collective-permute-start | bytes 1867784 | tf_op jit(solution)/shard_map/near/ppermute | solution.py:35
  19.7 2.2 %collective-permute-start.3 = (s32[1,1024]{1,0:T(1,128)S(1)}, s32[1,1024]{1,0:T(1,128)S(1)}, u32[]{:S(2)}, u32[]{:S(2)}) collective-permute-start(s32[1,1024]{1,0:T(1,128)S(1)} %copy-done.5), channel_id=1, source_target_pairs={{0,128},{1,97},{2,66},{3,163},{4,132},{5,101},{6,70},{7,167},{8,13... | collective-permute-start | bytes 12296 | tf_op jit(solution)/shard_map/idx_2/ppermute | solution.py:35
  22.0 7.9 %shard_map.106 = (bf16[304,1024]{1,0:T(8,128)(2,1)S(1)}, f32[304,1024]{1,0:T(8,128)}) custom-call(s32[1]{0:T(128)} %bitcast.swap_ref, s32[2,1024,1024]{2,1,0:T(8,128)} %bitcast.18, bf16[304,1024]{1,0:T(8,128)(2,1)} %get-tuple-element.28.row_ref, s32[1,1,2,1024]{3,2,1,0:T(2,128)S(1)} %copy-done, bf16[304,1024]{1,0:T(8,128)(2,1)S(1)} %collective-permute-done.block_ref), custom_call_target="tpu_custom_call" | custom-call | flops 3825205248 | bytes 12000000 | tf_op jit(solution)/shard_map/pallas_call | solution.py:187
  29.8 6.9 %collective-permute-done.3.idx_ref = s32[1,1024]{1,0:T(1,128)S(1)} collective-permute-done((s32[1,1024]{1,0:T(1,128)S(1)}, s32[1,1024]{1,0:T(1,128)S(1)}, u32[]{:S(2)}, u32[]{:S(2)}) %collective-permute-start.3) | collective-permute-done | bytes 4128 | tf_op jit(solution)/shard_map/idx_2/ppermute | solution.py:35
  36.7 2.6 %collective-permute-done.1.block_2_ref = bf16[304,1024]{1,0:T(8,128)(2,1)S(1)} collective-permute-done((bf16[304,1024]{1,0:T(8,128)(2,1)S(1)}, bf16[304,1024]{1,0:T(8,128)(2,1)S(1)}, u32[]{:S(2)}, u32[]{:S(2)}) %collective-permute-start.1) | collective-permute-done | bytes 622624 | tf_op jit(solution)/shard_map/near/ppermute | solution.py:35
  39.3 7.8 %shard_map.107 = (bf16[160,1024]{1,0:T(8,128)(2,1)S(1)}, bf16[144,1024]{1,0:T(8,128)(2,1)S(1)}, bf16[160,1024]{1,0:T(8,128)(2,1)S(1)}, bf16[160,1024]{1,0:T(8,128)(2,1)S(1)}) custom-call(s32[1]{0:T(128)} %bitcast.swap_ref, s32[2,1024,1024]{2,1,0:T(8,128)} %bitcast.19, bf16[304,1024]{1,0:T(8,128)(2,1)} %get-tuple-element.31.row_ref, ...), custom_call_target="tpu_custom_call" | custom-call | flops 3825205248 | bytes 12000000 | tf_op jit(solution)/shard_map/pallas_call | solution.py:222
  47.2 3.0 %collective-permute-start.7 = (bf16[160,1024]{1,0:T(8,128)(2,1)S(1)}, bf16[160,1024]{1,0:T(8,128)(2,1)S(1)}, u32[]{:S(2)}, u32[]{:S(2)}) collective-permute-start(bf16[160,1024]{1,0:T(8,128)(2,1)S(1)} %broadcast_select_fusion.1), channel_id=1, source_target_pairs={{0,1},{1,0},{2,3},{3,2},{4,5},{5,4},{6,7},{7,6},{8,9},{9,8},{10,11... | collective-permute-start | bytes 983048 | tf_op jit(solution)/shard_map/row_swap/ppermute | solution.py:35
  50.3 2.9 %collective-permute-start.4 = (bf16[160,1024]{1,0:T(8,128)(2,1)S(1)}, bf16[160,1024]{1,0:T(8,128)(2,1)S(1)}, u32[]{:S(2)}, u32[]{:S(2)}) collective-permute-start(bf16[160,1024]{1,0:T(8,128)(2,1)S(1)} %get-tuple-element.36), channel_id=1, source_target_pairs={{0,97},{1,160},{2,227},{3,34},{4,101},{5,164},{6,231},{7,38},{8,10... | collective-permute-start | bytes 983048 | tf_op jit(solution)/shard_map/low/ppermute | solution.py:35
  53.1 1.9 %collective-permute-start.6 = (bf16[144,1024]{1,0:T(8,128)(2,1)S(1)}, bf16[144,1024]{1,0:T(8,128)(2,1)S(1)}, u32[]{:S(2)}, u32[]{:S(2)}) collective-permute-start(bf16[144,1024]{1,0:T(8,128)(2,1)S(1)} %get-tuple-element.37), channel_id=1, source_target_pairs={{0,97},{1,160},{2,227},{3,34},{4,101},{5,164},{6,231},{7,38},{8,10... | collective-permute-start | bytes 884744 | tf_op jit(solution)/shard_map/high/ppermute | solution.py:35
  55.6 15.1 %collective-permute-done.4 = bf16[160,1024]{1,0:T(8,128)(2,1)S(1)} collective-permute-done((bf16[160,1024]{1,0:T(8,128)(2,1)S(1)}, bf16[160,1024]{1,0:T(8,128)(2,1)S(1)}, u32[]{:S(2)}, u32[]{:S(2)}) %collective-permute-start.4) | collective-permute-done | bytes 327712 | tf_op jit(solution)/shard_map/low/ppermute | solution.py:35
  70.8 1.3 %collective-permute-start.5 = (bf16[160,1024]{1,0:T(8,128)(2,1)S(1)}, bf16[160,1024]{1,0:T(8,128)(2,1)S(1)}, u32[]{:S(2)}, u32[]{:S(2)}) collective-permute-start(bf16[160,1024]{1,0:T(8,128)(2,1)S(1)} %add_convert_fusion.4), channel_id=1, source_target_pairs={{1,32},{2,66},{5,36},{6,70},{9,40},{10,74},{13,44},{14,78},{17,48}... | collective-permute-start | bytes 983048 | tf_op jit(solution)/shard_map/low_up/ppermute | solution.py:35
  72.9 3.0 %collective-permute-done.6 = bf16[144,1024]{1,0:T(8,128)(2,1)S(1)} collective-permute-done((bf16[144,1024]{1,0:T(8,128)(2,1)S(1)}, bf16[144,1024]{1,0:T(8,128)(2,1)S(1)}, u32[]{:S(2)}, u32[]{:S(2)}) %collective-permute-start.6) | collective-permute-done | bytes 294944 | tf_op jit(solution)/shard_map/high/ppermute | solution.py:35
  76.0 3.5 %collective-permute-start.13 = (bf16[144,1024]{1,0:T(8,128)(2,1)S(1)}, bf16[144,1024]{1,0:T(8,128)(2,1)S(1)}, u32[]{:S(2)}, u32[]{:S(2)}) collective-permute-start(bf16[144,1024]{1,0:T(8,128)(2,1)S(1)} %add_convert_fusion.7), channel_id=1, source_target_pairs={{1,32},{2,67},{5,36},{6,71},{9,40},{10,75},{13,44},{14,79},{17,48}... | collective-permute-start | bytes 884744 | tf_op jit(solution)/shard_map/high_up/ppermute | solution.py:35
  84.1 1.2 %fusion.2 = bf16[300,1024]{1,0:T(8,128)(2,1)} fusion(f32[1024,300]{0,1:T(8,128)S(1)} %copy-done.2, bf16[140,1024]{1,0:T(8,128)(2,1)S(1)} %slice_select_fusion, bf16[160,1024]{1,0:T(8,128)(2,1)S(1)} %broadcast_select_fusion, bf16[1024,300]{0,1:T(8,128)(2,1)S(1)} %copy-done.4), kind=kLoop, calls=%fused_computation.6 | loop fusion | flops 3379200 | bytes 3072000 | tf_op jit(solution)/shard_map/convert_element_type | solution.py:236
  85.4 1.4 %collective-permute-start.12 = (bf16[160,1024]{1,0:T(8,128)(2,1)S(1)}, bf16[160,1024]{1,0:T(8,128)(2,1)S(1)}, u32[]{:S(2)}, u32[]{:S(2)}) collective-permute-start(bf16[160,1024]{1,0:T(8,128)(2,1)S(1)} %add_convert_fusion), channel_id=1, source_target_pairs={{0,1},{2,3},{4,5},{6,7},{8,9},{10,11},{12,13},{14,15},{16,17},{18,... | collective-permute-start | bytes 983048 | tf_op jit(solution)/shard_map/low_other/ppermute | solution.py:35
  86.9 1.3 %collective-permute-start.16 = (bf16[144,1024]{1,0:T(8,128)(2,1)S(1)}, bf16[144,1024]{1,0:T(8,128)(2,1)S(1)}, u32[]{:S(2)}, u32[]{:S(2)}) collective-permute-start(bf16[144,1024]{1,0:T(8,128)(2,1)S(1)} %add_convert_fusion.5), channel_id=1, source_target_pairs={{0,1},{3,2},{4,5},{7,6},{8,9},{11,10},{12,13},{15,14},{16,17},{19,... | collective-permute-start | bytes 884744 | tf_op jit(solution)/shard_map/high_other/ppermute | solution.py:35
  88.2 7.9 %collective-permute-done.12 = bf16[160,1024]{1,0:T(8,128)(2,1)S(1)} collective-permute-done((bf16[160,1024]{1,0:T(8,128)(2,1)S(1)}, bf16[160,1024]{1,0:T(8,128)(2,1)S(1)}, u32[]{:S(2)}, u32[]{:S(2)}) %collective-permute-start.12) | collective-permute-done | bytes 327712 | tf_op jit(solution)/shard_map/low_other/ppermute | solution.py:35
  96.2 1.6 %collective-permute-done.16 = bf16[144,1024]{1,0:T(8,128)(2,1)S(1)} collective-permute-done((bf16[144,1024]{1,0:T(8,128)(2,1)S(1)}, bf16[144,1024]{1,0:T(8,128)(2,1)S(1)}, u32[]{:S(2)}, u32[]{:S(2)}) %collective-permute-start.16) | collective-permute-done | bytes 294944 | tf_op jit(solution)/shard_map/high_other/ppermute | solution.py:35
  97.8 1.2 %fusion.10 = bf16[1024,300]{0,1:T(8,128)(2,1)} fusion(f32[1024,300]{0,1:T(8,128)S(1)} %copy-done.3, bf16[140,1024]{1,0:T(8,128)(2,1)S(1)} %slice_add_fusion, bf16[160,1024]{1,0:T(8,128)(2,1)S(1)} %add.50, bf16[1024,300]{0,1:T(8,128)(2,1)S(1)} %copy-done.1), kind=kLoop, calls=%fused_computation.19 | loop fusion | flops 3379200 | bytes 3072000 | tf_op jit(solution)/shard_map/transpose | solution.py:305
  (41 shorter events, 6.3 us)
Async XLA Ops:
  2.6 15.8 %collective-permute-start = (bf16[304,1024]{1,0:T(8,128)(2,1)}, bf16[304,1024]{1,0:T(8,128)(2,1)S(1)}, u32[]{:S(2)}, u32[]{:S(2)}) collective-permute-start(bf16[304,1024]{1,0:T(8,128)(2,1)} %get-tuple-element.24), channel_id=1, source_target_pairs={{0,0},{1,225},{2,194},{3,35},{4,4},{5,229},{6,198},{7,39},{8,8},{9... | collective-permute-start | bytes 1867784 | tf_op jit(solution)/shard_map/got/ppermute | solution.py:35
  10.9 25.8 %collective-permute-start.2 = (bf16[304,1024]{1,0:T(8,128)(2,1)}, bf16[304,1024]{1,0:T(8,128)(2,1)S(1)}, u32[]{:S(2)}, u32[]{:S(2)}) collective-permute-start(bf16[304,1024]{1,0:T(8,128)(2,1)} %get-tuple-element.24), channel_id=1, source_target_pairs={{1,97},{5,101},{9,105},{13,109},{17,113},{21,117},{25,121},{29,125... | collective-permute-start | bytes 1867784 | tf_op jit(solution)/shard_map/far/ppermute | solution.py:35
  12.9 6.9 %copy-start.5 = (s32[1,1024]{1,0:T(1,128)S(1)}, s32[1,1024]{1,0:T(1,128)}, u32[]{:S(2)}) copy-start(s32[1,1024]{1,0:T(1,128)} %get-tuple-element.27) | copy-start | bytes 12292
  12.9 9.1 %copy-start = (s32[1,1,2,1024]{3,2,1,0:T(2,128)S(1)}, s32[1,1,2,1024]{3,2,1,0:T(2,128)}, u32[]{:S(2)}) copy-start(s32[1,1,2,1024]{3,2,1,0:T(2,128)} %row_idx_ref.3) | copy-start | bytes 24580
  18.4 20.9 %collective-permute-start.1 = (bf16[304,1024]{1,0:T(8,128)(2,1)S(1)}, bf16[304,1024]{1,0:T(8,128)(2,1)S(1)}, u32[]{:S(2)}, u32[]{:S(2)}) collective-permute-start(bf16[304,1024]{1,0:T(8,128)(2,1)S(1)} %collective-permute-done.block_ref), channel_id=1, source_target_pairs={{1,160},{2,227},{3,34},{5,164},{6,231},{7,38},{9,168},{10,235},{11... | collective-permute-start | bytes 1867784 | tf_op jit(solution)/shard_map/near/ppermute | solution.py:35
  19.7 17.0 %collective-permute-start.3 = (s32[1,1024]{1,0:T(1,128)S(1)}, s32[1,1024]{1,0:T(1,128)S(1)}, u32[]{:S(2)}, u32[]{:S(2)}) collective-permute-start(s32[1,1024]{1,0:T(1,128)S(1)} %copy-done.5), channel_id=1, source_target_pairs={{0,128},{1,97},{2,66},{3,163},{4,132},{5,101},{6,70},{7,167},{8,13... | collective-permute-start | bytes 12296 | tf_op jit(solution)/shard_map/idx_2/ppermute | solution.py:35
  47.2 7.8 %collective-permute-start.7 = (bf16[160,1024]{1,0:T(8,128)(2,1)S(1)}, bf16[160,1024]{1,0:T(8,128)(2,1)S(1)}, u32[]{:S(2)}, u32[]{:S(2)}) collective-permute-start(bf16[160,1024]{1,0:T(8,128)(2,1)S(1)} %broadcast_select_fusion.1), channel_id=1, source_target_pairs={{0,1},{1,0},{2,3},{3,2},{4,5},{5,4},{6,7},{7,6},{8,9},{9,8},{10,11... | collective-permute-start | bytes 983048 | tf_op jit(solution)/shard_map/row_swap/ppermute | solution.py:35
  50.3 20.5 %collective-permute-start.4 = (bf16[160,1024]{1,0:T(8,128)(2,1)S(1)}, bf16[160,1024]{1,0:T(8,128)(2,1)S(1)}, u32[]{:S(2)}, u32[]{:S(2)}) collective-permute-start(bf16[160,1024]{1,0:T(8,128)(2,1)S(1)} %get-tuple-element.36), channel_id=1, source_target_pairs={{0,97},{1,160},{2,227},{3,34},{4,101},{5,164},{6,231},{7,38},{8,10... | collective-permute-start | bytes 983048 | tf_op jit(solution)/shard_map/low/ppermute | solution.py:35
  53.1 22.8 %collective-permute-start.6 = (bf16[144,1024]{1,0:T(8,128)(2,1)S(1)}, bf16[144,1024]{1,0:T(8,128)(2,1)S(1)}, u32[]{:S(2)}, u32[]{:S(2)}) collective-permute-start(bf16[144,1024]{1,0:T(8,128)(2,1)S(1)} %get-tuple-element.37), channel_id=1, source_target_pairs={{0,97},{1,160},{2,227},{3,34},{4,101},{5,164},{6,231},{7,38},{8,10... | collective-permute-start | bytes 884744 | tf_op jit(solution)/shard_map/high/ppermute | solution.py:35
  55.2 20.8 %collective-permute-start.8 = (bf16[160,1024]{1,0:T(8,128)(2,1)S(1)}, bf16[160,1024]{1,0:T(8,128)(2,1)S(1)}, u32[]{:S(2)}, u32[]{:S(2)}) collective-permute-start(bf16[160,1024]{1,0:T(8,128)(2,1)S(1)} %add_convert_fusion.3), channel_id=1, source_target_pairs={{0,2},{1,3},{2,0},{3,1},{4,6},{5,7},{6,4},{7,5},{8,10},{9,11},{10,... | collective-permute-start | bytes 983048 | tf_op jit(solution)/shard_map/row_across/ppermute | solution.py:35
  70.8 9.3 %collective-permute-start.5 = (bf16[160,1024]{1,0:T(8,128)(2,1)S(1)}, bf16[160,1024]{1,0:T(8,128)(2,1)S(1)}, u32[]{:S(2)}, u32[]{:S(2)}) collective-permute-start(bf16[160,1024]{1,0:T(8,128)(2,1)S(1)} %add_convert_fusion.4), channel_id=1, source_target_pairs={{1,32},{2,66},{5,36},{6,70},{9,40},{10,74},{13,44},{14,78},{17,48}... | collective-permute-start | bytes 983048 | tf_op jit(solution)/shard_map/low_up/ppermute | solution.py:35
  72.2 9.2 %collective-permute-start.9 = (bf16[160,1024]{1,0:T(8,128)(2,1)S(1)}, bf16[160,1024]{1,0:T(8,128)(2,1)S(1)}, u32[]{:S(2)}, u32[]{:S(2)}) collective-permute-start(bf16[160,1024]{1,0:T(8,128)(2,1)S(1)} %add_convert_fusion.4), channel_id=1, source_target_pairs={{3,226},{7,230},{11,234},{15,238},{19,242},{23,246},{27,250},{31,2... | collective-permute-start | bytes 983048 | tf_op jit(solution)/shard_map/low_down/ppermute | solution.py:35
  76.0 7.1 %collective-permute-start.13 = (bf16[144,1024]{1,0:T(8,128)(2,1)S(1)}, bf16[144,1024]{1,0:T(8,128)(2,1)S(1)}, u32[]{:S(2)}, u32[]{:S(2)}) collective-permute-start(bf16[144,1024]{1,0:T(8,128)(2,1)S(1)} %add_convert_fusion.7), channel_id=1, source_target_pairs={{1,32},{2,67},{5,36},{6,71},{9,40},{10,75},{13,44},{14,79},{17,48}... | collective-permute-start | bytes 884744 | tf_op jit(solution)/shard_map/high_up/ppermute | solution.py:35
  79.5 3.6 %collective-permute-start.14 = (bf16[144,1024]{1,0:T(8,128)(2,1)S(1)}, bf16[144,1024]{1,0:T(8,128)(2,1)S(1)}, u32[]{:S(2)}, u32[]{:S(2)}) collective-permute-start(bf16[144,1024]{1,0:T(8,128)(2,1)S(1)} %add_convert_fusion.7), channel_id=1, source_target_pairs={{3,227},{7,231},{11,235},{15,239},{19,243},{23,247},{27,251},{31,2... | collective-permute-start | bytes 884744 | tf_op jit(solution)/shard_map/high_down/ppermute | solution.py:35
  80.3 3.7 %collective-permute-start.11 = (bf16[160,1024]{1,0:T(8,128)(2,1)S(1)}, bf16[160,1024]{1,0:T(8,128)(2,1)S(1)}, u32[]{:S(2)}, u32[]{:S(2)}) collective-permute-start(bf16[160,1024]{1,0:T(8,128)(2,1)S(1)} %add_convert_fusion.1), channel_id=1, source_target_pairs={{0,1},{1,0},{2,3},{3,2},{4,5},{5,4},{6,7},{7,6},{8,9},{9,8},{10,11... | collective-permute-start | bytes 983048 | tf_op jit(solution)/shard_map/row_other/ppermute | solution.py:35
  81.5 2.5 %copy-start.2 = (f32[1024,300]{0,1:T(8,128)S(1)}, f32[1024,300]{0,1:T(8,128)}, u32[]{:S(2)}) copy-start(f32[1024,300]{0,1:T(8,128)} %param.11) | copy-start | bytes 3686404
  81.6 2.5 %copy-start.4 = (bf16[1024,300]{0,1:T(8,128)(2,1)S(1)}, bf16[1024,300]{0,1:T(8,128)(2,1)}, u32[]{:S(2)}) copy-start(bf16[1024,300]{0,1:T(8,128)(2,1)} %param.9) | copy-start | bytes 1843204
  81.6 3.7 %collective-permute-start.10 = (bf16[160,1024]{1,0:T(8,128)(2,1)S(1)}, bf16[160,1024]{1,0:T(8,128)(2,1)S(1)}, u32[]{:S(2)}, u32[]{:S(2)}) collective-permute-start(bf16[160,1024]{1,0:T(8,128)(2,1)S(1)} %add_convert_fusion.2), channel_id=1, source_target_pairs={{0,2},{2,0},{4,6},{6,4},{8,10},{10,8},{12,14},{14,12},{16,18},{18,... | collective-permute-start | bytes 983048 | tf_op jit(solution)/shard_map/low_across/ppermute | solution.py:35
  83.3 3.6 %collective-permute-start.15 = (bf16[144,1024]{1,0:T(8,128)(2,1)S(1)}, bf16[144,1024]{1,0:T(8,128)(2,1)S(1)}, u32[]{:S(2)}, u32[]{:S(2)}) collective-permute-start(bf16[144,1024]{1,0:T(8,128)(2,1)S(1)} %add_convert_fusion.6), channel_id=1, source_target_pairs={{0,3},{3,0},{4,7},{7,4},{8,11},{11,8},{12,15},{15,12},{16,19},{19,... | collective-permute-start | bytes 884744 | tf_op jit(solution)/shard_map/high_across/ppermute | solution.py:35
  85.4 12.4 %copy-start.1 = (bf16[1024,300]{0,1:T(8,128)(2,1)S(1)}, bf16[1024,300]{0,1:T(8,128)(2,1)}, u32[]{:S(2)}) copy-start(bf16[1024,300]{0,1:T(8,128)(2,1)} %param.10) | copy-start | bytes 1843204
  85.4 12.4 %copy-start.3 = (f32[1024,300]{0,1:T(8,128)S(1)}, f32[1024,300]{0,1:T(8,128)}, u32[]{:S(2)}) copy-start(f32[1024,300]{0,1:T(8,128)} %param.12) | copy-start | bytes 3686404
  85.4 10.7 %collective-permute-start.12 = (bf16[160,1024]{1,0:T(8,128)(2,1)S(1)}, bf16[160,1024]{1,0:T(8,128)(2,1)S(1)}, u32[]{:S(2)}, u32[]{:S(2)}) collective-permute-start(bf16[160,1024]{1,0:T(8,128)(2,1)S(1)} %add_convert_fusion), channel_id=1, source_target_pairs={{0,1},{2,3},{4,5},{6,7},{8,9},{10,11},{12,13},{14,15},{16,17},{18,... | collective-permute-start | bytes 983048 | tf_op jit(solution)/shard_map/low_other/ppermute | solution.py:35
  86.9 10.8 %collective-permute-start.16 = (bf16[144,1024]{1,0:T(8,128)(2,1)S(1)}, bf16[144,1024]{1,0:T(8,128)(2,1)S(1)}, u32[]{:S(2)}, u32[]{:S(2)}) collective-permute-start(bf16[144,1024]{1,0:T(8,128)(2,1)S(1)} %add_convert_fusion.5), channel_id=1, source_target_pairs={{0,1},{3,2},{4,5},{7,6},{8,9},{11,10},{12,13},{15,14},{16,17},{19,... | collective-permute-start | bytes 884744 | tf_op jit(solution)/shard_map/high_other/ppermute | solution.py:35

commit v4 on v3

--- a/solution.py
+++ b/solution.py
@@ -140,16 +140,23 @@
     return copy
 
 
-def score(pair, idx, block, counts_ref, row_ref, row_idx, counts, row, cell_buf, sems):
+def score(pair, idx, block, counts_ref, row_ref, row_idx, counts, row, cell_buf, sems, then=None):
     get_row = start(row_ref, row, sems.at[0])
-    get_counts = start(counts_ref.at[pair], counts, sems.at[1])
+    parts = [pl.ds(i * (TERMS // 4), TERMS // 4) for i in range(4)]
+    get_counts = [
+        start(counts_ref.at[pair, part], counts.at[part], sems.at[4 + i])
+        for i, part in enumerate(parts)
+    ]
     pick = one_hot(idx)
     col = dot(block, pick, 1, 0)
     at = lax.broadcasted_iota(jnp.int32, (WIDE, TERMS), 0)
     col = jnp.where(at > OFF, jnp.where(at == ONE, 1.0, 0.0), col).astype(BF16)
     get_row.wait()
     est = dot(row[...], col, 0, 0)
-    get_counts.wait()
+    for get in get_counts:
+        get.wait()
+    if then is not None:
+        then()
     cell_buf[...] = cells(est, counts[...])
     grad = dot(row[...], cell_buf[...], 1, 0).astype(BF16)
     grad = dot(grad, pick, 1, 1).astype(BF16)
@@ -161,7 +168,7 @@
     pltpu.VMEM((TERMS, TERMS), jnp.int32),
     pltpu.VMEM((WIDE, TERMS), BF16),
     pltpu.VMEM((TERMS, TERMS), BF16),
-    pltpu.SemaphoreType.DMA((3,)),
+    pltpu.SemaphoreType.DMA((8,)),
     pltpu.VMEM((WIDE, TERMS), F32),
 ]
 
@@ -206,11 +213,12 @@
     low_out, high_out, row_low_out, row_high_out, counts, row, cell_buf, sems, prev,
 ):
     swap = swap_ref[0]
-    get_prev = start(prev_ref, prev, sems.at[2])
+    get_prev = pltpu.make_async_copy(prev_ref, prev, sems.at[2])
     row_idx = order(row_idx_ref, swap == 1)[1]
     block = block_ref[...] + block_2_ref[...]
     grad, total = score(
-        1 - swap, idx_ref[...], block, counts_ref, row_ref, row_idx, counts, row, cell_buf, sems
+        1 - swap, idx_ref[...], block, counts_ref, row_ref, row_idx, counts, row, cell_buf, sems,
+        get_prev.start,
     )
     low_out[...] = grad[:LOW]
     high_out[...] = grad[LOW:]

time: 99.5 us -> 99.4 us (level)
  waiting for transfers between devices: 39.9 us -> 38.2 us
  starting transfers between devices: 33.4 us -> 34.4 us
    ppermute x17, waiting for transfers between devices: 39.9 us -> 38.2 us  [hop(): return lax.ppermute(array, AXES, perm)]
  transfers between devices with their start and end apart: 17 -> 17, of which waited for: 8 -> 8; matrix products, arithmetic and copies ran while one was open for 2% -> 2% of each run, Pallas kernels for 11% -> 12%
where the time goes in v4:
time: 99.4 us; the launch traced here: 99 us
  waiting for transfers between devices  38.2 us (38%)
  starting transfers between devices  34.4 us (35%)
  Pallas kernels  21.9 us (22%)
  other arithmetic  3.56 us (4%)
    ppermute x17, waiting for transfers between devices, hop(): return lax.ppermute(array, AXES, perm)  38.2 us
    ppermute x17, starting transfers between devices, hop(): return lax.ppermute(array, AXES, perm)  34.4 us
    pallas_call x1, Pallas kernels, first_pair(): pl.pallas_call(first_kernel, out_shape=(vmem(WIDE), pltpu.HBM((WIDE, TERM...  8.7 us
    pallas_call x1, Pallas kernels, second_pair(): pl.pallas_call(second_kernel, out_shape=(vmem(LOW), vmem(HIGH), shape(LOW...  7.78 us
    pallas_call x1, Pallas kernels, pick_rows(): pl.pallas_call(rows_kernel, out_shape=(shape(WIDE), shape(WIDE)), in_spec...  3.44 us
  transfers between devices with their start and end apart: 17, of which 8 were waited for; matrix products, arithmetic and copies ran while one was open for 2% of the time, Pallas kernels for 12%

profile of v4, /device:TPU:1, one launch (start us, length us, event | category | flops | bytes accessed | tf_op | source)
XLA Modules:
  0.0 99.0 jit_solution(8809077875687443748)
XLA Ops:
  0.6 2.0 %shard_map.104 = (bf16[304,1024]{1,0:T(8,128)(2,1)}, s32[1,1024]{1,0:T(1,128)}) custom-call(s32[1]{0:T(128)} %bitcast.swap_ref, bf16[300,1024]{1,0:T(8,128)(2,1)} %bitcast.15, bf16[1024]{0:T(1024)(128)(2,1)} %off_ref.2, s32[1,1,2,1024]{3,2,1,0:T(2,128)} %idx_ref.2), custom_call_target="tpu_custom_call" | custom-call | bytes 1300000 | tf_op jit(solution)/shard_map/pallas_call | solution.py:98
  2.6 8.3 %collective-permute-start = (bf16[304,1024]{1,0:T(8,128)(2,1)}, bf16[304,1024]{1,0:T(8,128)(2,1)S(1)}, u32[]{:S(2)}, u32[]{:S(2)}) collective-permute-start(bf16[304,1024]{1,0:T(8,128)(2,1)} %get-tuple-element.24), channel_id=1, source_target_pairs={{0,0},{1,225},{2,194},{3,35},{4,4},{5,229},{6,198},{7,39},{8,8},{9... | collective-permute-start | bytes 1867784 | tf_op jit(solution)/shard_map/got/ppermute | solution.py:35
  10.9 1.9 %collective-permute-start.2 = (bf16[304,1024]{1,0:T(8,128)(2,1)}, bf16[304,1024]{1,0:T(8,128)(2,1)S(1)}, u32[]{:S(2)}, u32[]{:S(2)}) collective-permute-start(bf16[304,1024]{1,0:T(8,128)(2,1)} %get-tuple-element.24), channel_id=1, source_target_pairs={{1,97},{5,101},{9,105},{13,109},{17,113},{21,117},{25,121},{29,125... | collective-permute-start | bytes 1867784 | tf_op jit(solution)/shard_map/far/ppermute | solution.py:35
  12.9 3.4 %shard_map.105 = (bf16[304,1024]{1,0:T(8,128)(2,1)}, bf16[304,1024]{1,0:T(8,128)(2,1)}) custom-call(s32[1]{0:T(128)} %bitcast.swap_ref, bf16[300,1024]{1,0:T(8,128)(2,1)} %bitcast.16, bf16[1024]{0:T(1024)(128)(2,1)} %off_ref.3, s32[1,1,2,1024]{3,2,1,0:T(2,128)} %row_idx_ref.3), custom_call_target="tpu_custom_call" | custom-call | flops 1275068416 | bytes 2000000 | tf_op jit(solution)/shard_map/pallas_call | solution.py:118
  16.3 2.1 %collective-permute-done.block_ref = bf16[304,1024]{1,0:T(8,128)(2,1)S(1)} collective-permute-done((bf16[304,1024]{1,0:T(8,128)(2,1)}, bf16[304,1024]{1,0:T(8,128)(2,1)S(1)}, u32[]{:S(2)}, u32[]{:S(2)}) %collective-permute-start) | collective-permute-done | bytes 622624 | tf_op jit(solution)/shard_map/got/ppermute | solution.py:35
  18.4 1.3 %collective-permute-start.1 = (bf16[304,1024]{1,0:T(8,128)(2,1)S(1)}, bf16[304,1024]{1,0:T(8,128)(2,1)S(1)}, u32[]{:S(2)}, u32[]{:S(2)}) collective-permute-start(bf16[304,1024]{1,0:T(8,128)(2,1)S(1)} %collective-permute-done.block_ref), channel_id=1, source_target_pairs={{1,160},{2,227},{3,34},{5,164},{6,231},{7,38},{9,168},{10,235},{11... | collective-permute-start | bytes 1867784 | tf_op jit(solution)/shard_map/near/ppermute | solution.py:35
  19.7 2.2 %collective-permute-start.3 = (s32[1,1024]{1,0:T(1,128)S(1)}, s32[1,1024]{1,0:T(1,128)S(1)}, u32[]{:S(2)}, u32[]{:S(2)}) collective-permute-start(s32[1,1024]{1,0:T(1,128)S(1)} %copy-done.5), channel_id=1, source_target_pairs={{0,128},{1,97},{2,66},{3,163},{4,132},{5,101},{6,70},{7,167},{8,13... | collective-permute-start | bytes 12296 | tf_op jit(solution)/shard_map/idx_2/ppermute | solution.py:35
  22.0 8.7 %shard_map.106 = (bf16[304,1024]{1,0:T(8,128)(2,1)S(1)}, f32[304,1024]{1,0:T(8,128)}) custom-call(s32[1]{0:T(128)} %bitcast.swap_ref, s32[2,1024,1024]{2,1,0:T(8,128)} %bitcast.18, bf16[304,1024]{1,0:T(8,128)(2,1)} %get-tuple-element.28.row_ref, s32[1,1,2,1024]{3,2,1,0:T(2,128)S(1)} %copy-done, bf16[304,1024]{1,0:T(8,128)(2,1)S(1)} %collective-permute-done.block_ref), custom_call_target="tpu_custom_call" | custom-call | flops 3825205248 | bytes 12000000 | tf_op jit(solution)/shard_map/pallas_call | solution.py:194
  30.7 6.0 %collective-permute-done.3.idx_ref = s32[1,1024]{1,0:T(1,128)S(1)} collective-permute-done((s32[1,1024]{1,0:T(1,128)S(1)}, s32[1,1024]{1,0:T(1,128)S(1)}, u32[]{:S(2)}, u32[]{:S(2)}) %collective-permute-start.3) | collective-permute-done | bytes 4128 | tf_op jit(solution)/shard_map/idx_2/ppermute | solution.py:35
  36.7 2.6 %collective-permute-done.1.block_2_ref = bf16[304,1024]{1,0:T(8,128)(2,1)S(1)} collective-permute-done((bf16[304,1024]{1,0:T(8,128)(2,1)S(1)}, bf16[304,1024]{1,0:T(8,128)(2,1)S(1)}, u32[]{:S(2)}, u32[]{:S(2)}) %collective-permute-start.1) | collective-permute-done | bytes 622624 | tf_op jit(solution)/shard_map/near/ppermute | solution.py:35
  39.3 7.8 %shard_map.107 = (bf16[160,1024]{1,0:T(8,128)(2,1)S(1)}, bf16[144,1024]{1,0:T(8,128)(2,1)S(1)}, bf16[160,1024]{1,0:T(8,128)(2,1)S(1)}, bf16[160,1024]{1,0:T(8,128)(2,1)S(1)}) custom-call(s32[1]{0:T(128)} %bitcast.swap_ref, s32[2,1024,1024]{2,1,0:T(8,128)} %bitcast.19, bf16[304,1024]{1,0:T(8,128)(2,1)} %get-tuple-element.31.row_ref, ...), custom_call_target="tpu_custom_call" | custom-call | flops 3825205248 | bytes 12000000 | tf_op jit(solution)/shard_map/pallas_call | solution.py:230
  47.2 3.1 %collective-permute-start.7 = (bf16[160,1024]{1,0:T(8,128)(2,1)S(1)}, bf16[160,1024]{1,0:T(8,128)(2,1)S(1)}, u32[]{:S(2)}, u32[]{:S(2)}) collective-permute-start(bf16[160,1024]{1,0:T(8,128)(2,1)S(1)} %broadcast_select_fusion.1), channel_id=1, source_target_pairs={{0,1},{1,0},{2,3},{3,2},{4,5},{5,4},{6,7},{7,6},{8,9},{9,8},{10,11... | collective-permute-start | bytes 983048 | tf_op jit(solution)/shard_map/row_swap/ppermute | solution.py:35
  50.2 2.9 %collective-permute-start.4 = (bf16[160,1024]{1,0:T(8,128)(2,1)S(1)}, bf16[160,1024]{1,0:T(8,128)(2,1)S(1)}, u32[]{:S(2)}, u32[]{:S(2)}) collective-permute-start(bf16[160,1024]{1,0:T(8,128)(2,1)S(1)} %get-tuple-element.36), channel_id=1, source_target_pairs={{0,97},{1,160},{2,227},{3,34},{4,101},{5,164},{6,231},{7,38},{8,10... | collective-permute-start | bytes 983048 | tf_op jit(solution)/shard_map/low/ppermute | solution.py:35
  53.1 1.9 %collective-permute-start.6 = (bf16[144,1024]{1,0:T(8,128)(2,1)S(1)}, bf16[144,1024]{1,0:T(8,128)(2,1)S(1)}, u32[]{:S(2)}, u32[]{:S(2)}) collective-permute-start(bf16[144,1024]{1,0:T(8,128)(2,1)S(1)} %get-tuple-element.37), channel_id=1, source_target_pairs={{0,97},{1,160},{2,227},{3,34},{4,101},{5,164},{6,231},{7,38},{8,10... | collective-permute-start | bytes 884744 | tf_op jit(solution)/shard_map/high/ppermute | solution.py:35
  55.1 1.3 %collective-permute-start.8 = (bf16[160,1024]{1,0:T(8,128)(2,1)S(1)}, bf16[160,1024]{1,0:T(8,128)(2,1)S(1)}, u32[]{:S(2)}, u32[]{:S(2)}) collective-permute-start(bf16[160,1024]{1,0:T(8,128)(2,1)S(1)} %add_convert_fusion.3), channel_id=1, source_target_pairs={{0,2},{1,3},{2,0},{3,1},{4,6},{5,7},{6,4},{7,5},{8,10},{9,11},{10,... | collective-permute-start | bytes 983048 | tf_op jit(solution)/shard_map/row_across/ppermute | solution.py:35
  56.4 14.3 %collective-permute-done.4 = bf16[160,1024]{1,0:T(8,128)(2,1)S(1)} collective-permute-done((bf16[160,1024]{1,0:T(8,128)(2,1)S(1)}, bf16[160,1024]{1,0:T(8,128)(2,1)S(1)}, u32[]{:S(2)}, u32[]{:S(2)}) %collective-permute-start.4) | collective-permute-done | bytes 327712 | tf_op jit(solution)/shard_map/low/ppermute | solution.py:35
  70.8 1.3 %collective-permute-start.5 = (bf16[160,1024]{1,0:T(8,128)(2,1)S(1)}, bf16[160,1024]{1,0:T(8,128)(2,1)S(1)}, u32[]{:S(2)}, u32[]{:S(2)}) collective-permute-start(bf16[160,1024]{1,0:T(8,128)(2,1)S(1)} %add_convert_fusion.4), channel_id=1, source_target_pairs={{1,32},{2,66},{5,36},{6,70},{9,40},{10,74},{13,44},{14,78},{17,48}... | collective-permute-start | bytes 983048 | tf_op jit(solution)/shard_map/low_up/ppermute | solution.py:35
  72.8 3.0 %collective-permute-done.6 = bf16[144,1024]{1,0:T(8,128)(2,1)S(1)} collective-permute-done((bf16[144,1024]{1,0:T(8,128)(2,1)S(1)}, bf16[144,1024]{1,0:T(8,128)(2,1)S(1)}, u32[]{:S(2)}, u32[]{:S(2)}) %collective-permute-start.6) | collective-permute-done | bytes 294944 | tf_op jit(solution)/shard_map/high/ppermute | solution.py:35
  75.9 3.7 %collective-permute-start.13 = (bf16[144,1024]{1,0:T(8,128)(2,1)S(1)}, bf16[144,1024]{1,0:T(8,128)(2,1)S(1)}, u32[]{:S(2)}, u32[]{:S(2)}) collective-permute-start(bf16[144,1024]{1,0:T(8,128)(2,1)S(1)} %add_convert_fusion.7), channel_id=1, source_target_pairs={{1,32},{2,67},{5,36},{6,71},{9,40},{10,75},{13,44},{14,79},{17,48}... | collective-permute-start | bytes 884744 | tf_op jit(solution)/shard_map/high_up/ppermute | solution.py:35
  84.1 1.2 %fusion.2 = bf16[300,1024]{1,0:T(8,128)(2,1)} fusion(f32[1024,300]{0,1:T(8,128)S(1)} %copy-done.2, bf16[140,1024]{1,0:T(8,128)(2,1)S(1)} %slice_select_fusion, bf16[160,1024]{1,0:T(8,128)(2,1)S(1)} %broadcast_select_fusion, bf16[1024,300]{0,1:T(8,128)(2,1)S(1)} %copy-done.4), kind=kLoop, calls=%fused_computation.6 | loop fusion | flops 3379200 | bytes 3072000 | tf_op jit(solution)/shard_map/convert_element_type | solution.py:244
  85.5 1.4 %collective-permute-start.12 = (bf16[160,1024]{1,0:T(8,128)(2,1)S(1)}, bf16[160,1024]{1,0:T(8,128)(2,1)S(1)}, u32[]{:S(2)}, u32[]{:S(2)}) collective-permute-start(bf16[160,1024]{1,0:T(8,128)(2,1)S(1)} %add_convert_fusion), channel_id=1, source_target_pairs={{0,1},{2,3},{4,5},{6,7},{8,9},{10,11},{12,13},{14,15},{16,17},{18,... | collective-permute-start | bytes 983048 | tf_op jit(solution)/shard_map/low_other/ppermute | solution.py:35
  87.0 1.3 %collective-permute-start.16 = (bf16[144,1024]{1,0:T(8,128)(2,1)S(1)}, bf16[144,1024]{1,0:T(8,128)(2,1)S(1)}, u32[]{:S(2)}, u32[]{:S(2)}) collective-permute-start(bf16[144,1024]{1,0:T(8,128)(2,1)S(1)} %add_convert_fusion.5), channel_id=1, source_target_pairs={{0,1},{3,2},{4,5},{7,6},{8,9},{11,10},{12,13},{15,14},{16,17},{19,... | collective-permute-start | bytes 884744 | tf_op jit(solution)/shard_map/high_other/ppermute | solution.py:35
  88.3 7.8 %collective-permute-done.12 = bf16[160,1024]{1,0:T(8,128)(2,1)S(1)} collective-permute-done((bf16[160,1024]{1,0:T(8,128)(2,1)S(1)}, bf16[160,1024]{1,0:T(8,128)(2,1)S(1)}, u32[]{:S(2)}, u32[]{:S(2)}) %collective-permute-start.12) | collective-permute-done | bytes 327712 | tf_op jit(solution)/shard_map/low_other/ppermute | solution.py:35
  96.2 1.6 %collective-permute-done.16 = bf16[144,1024]{1,0:T(8,128)(2,1)S(1)} collective-permute-done((bf16[144,1024]{1,0:T(8,128)(2,1)S(1)}, bf16[144,1024]{1,0:T(8,128)(2,1)S(1)}, u32[]{:S(2)}, u32[]{:S(2)}) %collective-permute-start.16) | collective-permute-done | bytes 294944 | tf_op jit(solution)/shard_map/high_other/ppermute | solution.py:35
  (41 shorter events, 7.1 us)
Async XLA Ops:
  2.6 15.8 %collective-permute-start = (bf16[304,1024]{1,0:T(8,128)(2,1)}, bf16[304,1024]{1,0:T(8,128)(2,1)S(1)}, u32[]{:S(2)}, u32[]{:S(2)}) collective-permute-start(bf16[304,1024]{1,0:T(8,128)(2,1)} %get-tuple-element.24), channel_id=1, source_target_pairs={{0,0},{1,225},{2,194},{3,35},{4,4},{5,229},{6,198},{7,39},{8,8},{9... | collective-permute-start | bytes 1867784 | tf_op jit(solution)/shard_map/got/ppermute | solution.py:35
  10.9 25.8 %collective-permute-start.2 = (bf16[304,1024]{1,0:T(8,128)(2,1)}, bf16[304,1024]{1,0:T(8,128)(2,1)S(1)}, u32[]{:S(2)}, u32[]{:S(2)}) collective-permute-start(bf16[304,1024]{1,0:T(8,128)(2,1)} %get-tuple-element.24), channel_id=1, source_target_pairs={{1,97},{5,101},{9,105},{13,109},{17,113},{21,117},{25,121},{29,125... | collective-permute-start | bytes 1867784 | tf_op jit(solution)/shard_map/far/ppermute | solution.py:35
  12.9 6.9 %copy-start.5 = (s32[1,1024]{1,0:T(1,128)S(1)}, s32[1,1024]{1,0:T(1,128)}, u32[]{:S(2)}) copy-start(s32[1,1024]{1,0:T(1,128)} %get-tuple-element.27) | copy-start | bytes 12292
  12.9 9.1 %copy-start = (s32[1,1,2,1024]{3,2,1,0:T(2,128)S(1)}, s32[1,1,2,1024]{3,2,1,0:T(2,128)}, u32[]{:S(2)}) copy-start(s32[1,1,2,1024]{3,2,1,0:T(2,128)} %row_idx_ref.3) | copy-start | bytes 24580
  18.4 20.9 %collective-permute-start.1 = (bf16[304,1024]{1,0:T(8,128)(2,1)S(1)}, bf16[304,1024]{1,0:T(8,128)(2,1)S(1)}, u32[]{:S(2)}, u32[]{:S(2)}) collective-permute-start(bf16[304,1024]{1,0:T(8,128)(2,1)S(1)} %collective-permute-done.block_ref), channel_id=1, source_target_pairs={{1,160},{2,227},{3,34},{5,164},{6,231},{7,38},{9,168},{10,235},{11... | collective-permute-start | bytes 1867784 | tf_op jit(solution)/shard_map/near/ppermute | solution.py:35
  19.7 17.0 %collective-permute-start.3 = (s32[1,1024]{1,0:T(1,128)S(1)}, s32[1,1024]{1,0:T(1,128)S(1)}, u32[]{:S(2)}, u32[]{:S(2)}) collective-permute-start(s32[1,1024]{1,0:T(1,128)S(1)} %copy-done.5), channel_id=1, source_target_pairs={{0,128},{1,97},{2,66},{3,163},{4,132},{5,101},{6,70},{7,167},{8,13... | collective-permute-start | bytes 12296 | tf_op jit(solution)/shard_map/idx_2/ppermute | solution.py:35
  47.2 7.8 %collective-permute-start.7 = (bf16[160,1024]{1,0:T(8,128)(2,1)S(1)}, bf16[160,1024]{1,0:T(8,128)(2,1)S(1)}, u32[]{:S(2)}, u32[]{:S(2)}) collective-permute-start(bf16[160,1024]{1,0:T(8,128)(2,1)S(1)} %broadcast_select_fusion.1), channel_id=1, source_target_pairs={{0,1},{1,0},{2,3},{3,2},{4,5},{5,4},{6,7},{7,6},{8,9},{9,8},{10,11... | collective-permute-start | bytes 983048 | tf_op jit(solution)/shard_map/row_swap/ppermute | solution.py:35
  50.2 20.5 %collective-permute-start.4 = (bf16[160,1024]{1,0:T(8,128)(2,1)S(1)}, bf16[160,1024]{1,0:T(8,128)(2,1)S(1)}, u32[]{:S(2)}, u32[]{:S(2)}) collective-permute-start(bf16[160,1024]{1,0:T(8,128)(2,1)S(1)} %get-tuple-element.36), channel_id=1, source_target_pairs={{0,97},{1,160},{2,227},{3,34},{4,101},{5,164},{6,231},{7,38},{8,10... | collective-permute-start | bytes 983048 | tf_op jit(solution)/shard_map/low/ppermute | solution.py:35
  53.1 22.7 %collective-permute-start.6 = (bf16[144,1024]{1,0:T(8,128)(2,1)S(1)}, bf16[144,1024]{1,0:T(8,128)(2,1)S(1)}, u32[]{:S(2)}, u32[]{:S(2)}) collective-permute-start(bf16[144,1024]{1,0:T(8,128)(2,1)S(1)} %get-tuple-element.37), channel_id=1, source_target_pairs={{0,97},{1,160},{2,227},{3,34},{4,101},{5,164},{6,231},{7,38},{8,10... | collective-permute-start | bytes 884744 | tf_op jit(solution)/shard_map/high/ppermute | solution.py:35
  55.1 20.7 %collective-permute-start.8 = (bf16[160,1024]{1,0:T(8,128)(2,1)S(1)}, bf16[160,1024]{1,0:T(8,128)(2,1)S(1)}, u32[]{:S(2)}, u32[]{:S(2)}) collective-permute-start(bf16[160,1024]{1,0:T(8,128)(2,1)S(1)} %add_convert_fusion.3), channel_id=1, source_target_pairs={{0,2},{1,3},{2,0},{3,1},{4,6},{5,7},{6,4},{7,5},{8,10},{9,11},{10,... | collective-permute-start | bytes 983048 | tf_op jit(solution)/shard_map/row_across/ppermute | solution.py:35
  70.8 9.4 %collective-permute-start.5 = (bf16[160,1024]{1,0:T(8,128)(2,1)S(1)}, bf16[160,1024]{1,0:T(8,128)(2,1)S(1)}, u32[]{:S(2)}, u32[]{:S(2)}) collective-permute-start(bf16[160,1024]{1,0:T(8,128)(2,1)S(1)} %add_convert_fusion.4), channel_id=1, source_target_pairs={{1,32},{2,66},{5,36},{6,70},{9,40},{10,74},{13,44},{14,78},{17,48}... | collective-permute-start | bytes 983048 | tf_op jit(solution)/shard_map/low_up/ppermute | solution.py:35
  72.1 9.2 %collective-permute-start.9 = (bf16[160,1024]{1,0:T(8,128)(2,1)S(1)}, bf16[160,1024]{1,0:T(8,128)(2,1)S(1)}, u32[]{:S(2)}, u32[]{:S(2)}) collective-permute-start(bf16[160,1024]{1,0:T(8,128)(2,1)S(1)} %add_convert_fusion.4), channel_id=1, source_target_pairs={{3,226},{7,230},{11,234},{15,238},{19,242},{23,246},{27,250},{31,2... | collective-permute-start | bytes 983048 | tf_op jit(solution)/shard_map/low_down/ppermute | solution.py:35
  75.9 7.3 %collective-permute-start.13 = (bf16[144,1024]{1,0:T(8,128)(2,1)S(1)}, bf16[144,1024]{1,0:T(8,128)(2,1)S(1)}, u32[]{:S(2)}, u32[]{:S(2)}) collective-permute-start(bf16[144,1024]{1,0:T(8,128)(2,1)S(1)} %add_convert_fusion.7), channel_id=1, source_target_pairs={{1,32},{2,67},{5,36},{6,71},{9,40},{10,75},{13,44},{14,79},{17,48}... | collective-permute-start | bytes 884744 | tf_op jit(solution)/shard_map/high_up/ppermute | solution.py:35
  79.5 3.6 %collective-permute-start.14 = (bf16[144,1024]{1,0:T(8,128)(2,1)S(1)}, bf16[144,1024]{1,0:T(8,128)(2,1)S(1)}, u32[]{:S(2)}, u32[]{:S(2)}) collective-permute-start(bf16[144,1024]{1,0:T(8,128)(2,1)S(1)} %add_convert_fusion.7), channel_id=1, source_target_pairs={{3,227},{7,231},{11,235},{15,239},{19,243},{23,247},{27,251},{31,2... | collective-permute-start | bytes 884744 | tf_op jit(solution)/shard_map/high_down/ppermute | solution.py:35
  80.3 3.7 %collective-permute-start.11 = (bf16[160,1024]{1,0:T(8,128)(2,1)S(1)}, bf16[160,1024]{1,0:T(8,128)(2,1)S(1)}, u32[]{:S(2)}, u32[]{:S(2)}) collective-permute-start(bf16[160,1024]{1,0:T(8,128)(2,1)S(1)} %add_convert_fusion.1), channel_id=1, source_target_pairs={{0,1},{1,0},{2,3},{3,2},{4,5},{5,4},{6,7},{7,6},{8,9},{9,8},{10,11... | collective-permute-start | bytes 983048 | tf_op jit(solution)/shard_map/row_other/ppermute | solution.py:35
  81.5 2.6 %copy-start.2 = (f32[1024,300]{0,1:T(8,128)S(1)}, f32[1024,300]{0,1:T(8,128)}, u32[]{:S(2)}) copy-start(f32[1024,300]{0,1:T(8,128)} %param.11) | copy-start | bytes 3686404
  81.5 2.6 %copy-start.4 = (bf16[1024,300]{0,1:T(8,128)(2,1)S(1)}, bf16[1024,300]{0,1:T(8,128)(2,1)}, u32[]{:S(2)}) copy-start(bf16[1024,300]{0,1:T(8,128)(2,1)} %param.9) | copy-start | bytes 1843204
  81.5 3.8 %collective-permute-start.10 = (bf16[160,1024]{1,0:T(8,128)(2,1)S(1)}, bf16[160,1024]{1,0:T(8,128)(2,1)S(1)}, u32[]{:S(2)}, u32[]{:S(2)}) collective-permute-start(bf16[160,1024]{1,0:T(8,128)(2,1)S(1)} %add_convert_fusion.2), channel_id=1, source_target_pairs={{0,2},{2,0},{4,6},{6,4},{8,10},{10,8},{12,14},{14,12},{16,18},{18,... | collective-permute-start | bytes 983048 | tf_op jit(solution)/shard_map/low_across/ppermute | solution.py:35
  83.3 3.6 %collective-permute-start.15 = (bf16[144,1024]{1,0:T(8,128)(2,1)S(1)}, bf16[144,1024]{1,0:T(8,128)(2,1)S(1)}, u32[]{:S(2)}, u32[]{:S(2)}) collective-permute-start(bf16[144,1024]{1,0:T(8,128)(2,1)S(1)} %add_convert_fusion.6), channel_id=1, source_target_pairs={{0,3},{3,0},{4,7},{7,4},{8,11},{11,8},{12,15},{15,12},{16,19},{19,... | collective-permute-start | bytes 884744 | tf_op jit(solution)/shard_map/high_across/ppermute | solution.py:35
  85.4 12.3 %copy-start.1 = (bf16[1024,300]{0,1:T(8,128)(2,1)S(1)}, bf16[1024,300]{0,1:T(8,128)(2,1)}, u32[]{:S(2)}) copy-start(bf16[1024,300]{0,1:T(8,128)(2,1)} %param.10) | copy-start | bytes 1843204
  85.5 12.3 %copy-start.3 = (f32[1024,300]{0,1:T(8,128)S(1)}, f32[1024,300]{0,1:T(8,128)}, u32[]{:S(2)}) copy-start(f32[1024,300]{0,1:T(8,128)} %param.12) | copy-start | bytes 3686404
  85.5 10.6 %collective-permute-start.12 = (bf16[160,1024]{1,0:T(8,128)(2,1)S(1)}, bf16[160,1024]{1,0:T(8,128)(2,1)S(1)}, u32[]{:S(2)}, u32[]{:S(2)}) collective-permute-start(bf16[160,1024]{1,0:T(8,128)(2,1)S(1)} %add_convert_fusion), channel_id=1, source_target_pairs={{0,1},{2,3},{4,5},{6,7},{8,9},{10,11},{12,13},{14,15},{16,17},{18,... | collective-permute-start | bytes 983048 | tf_op jit(solution)/shard_map/low_other/ppermute | solution.py:35
  87.0 10.8 %collective-permute-start.16 = (bf16[144,1024]{1,0:T(8,128)(2,1)S(1)}, bf16[144,1024]{1,0:T(8,128)(2,1)S(1)}, u32[]{:S(2)}, u32[]{:S(2)}) collective-permute-start(bf16[144,1024]{1,0:T(8,128)(2,1)S(1)} %add_convert_fusion.5), channel_id=1, source_target_pairs={{0,1},{3,2},{4,5},{7,6},{8,9},{11,10},{12,13},{15,14},{16,17},{19,... | collective-permute-start | bytes 884744 | tf_op jit(solution)/shard_map/high_other/ppermute | solution.py:35
